TPU v7x, 128 devices: a whole 4x4x4 slice. The times are simulated.
128 devices in a mesh: section: 2 (over core), tensor: 4 (over x), pool: 16 (over z, y).
Axes of the slice: x: 4, y: 4, z: 4, core: 2. Of those that a mesh axis runs over, the one named last changes fastest.
Arguments:
- hidden_input: bfloat16 [2, 512, 8192], P('section', None, 'pool'), may hold values from -6 to 6
- fresh: bfloat16 [512, 8192], P(None, 'pool'), may hold values from -6 to 6
- gain: float32 [2, 8192], P('section', 'pool'), may hold values from 0.5 to 1.5
- query_matrix: bfloat16 [2, 8192, 8192], P('section', 'pool', 'tensor'), may hold values from -0.0625 to 0.0625
- keyval_matrix: bfloat16 [2, 8192, 2, 1024], P('section', 'pool', None, 'tensor'), may hold values from -0.0625 to 0.0625
- output_weight: bfloat16 [2, 8192, 8192], P('section', 'tensor', 'pool'), may hold values from -0.0625 to 0.0625
- cache: bfloat16 [2, 2, 512, 128, 2, 1024], P('section', None, 'pool', None, None, 'tensor'), may hold values from -6 to 6
- lengths: int32 [3, 512], replicated, may hold values from 1 to 128, as said below
- adapter_of_row: int32 [3, 512], replicated, may hold values from 0 to 31
- adapters_per_batch: int32 [3, 32], replicated, may hold values from 0 to 255, as said below
- adapter_slot_table: int32 [256], replicated, may hold values from 0 to 255, as said below
- adapter_down: bfloat16 [256, 2, 16, 8192], P(('section', 'pool'), None, None, 'tensor'), may hold values from -0.0625 to 0.0625
- adapter_up: bfloat16 [256, 2, 16, 8192], P(('section', 'tensor'), None, None, 'pool'), may hold values from -1.5 to 1.5
Outputs:
- first_tick: bfloat16 [2, 512, 8192], P('section', 'tensor', 'pool')
- second_tick: bfloat16 [2, 512, 8192], P('section', 'tensor', 'pool')
Inputs may be any that keep to these rules, and one draw needn't show every extreme that they name: A permutation: adapter a's panels are row adapter_slot_table[a] of adapter_down and of adapter_up. `adapters_per_batch`: adapter numbers; the 32 adapters of a micro-batch have their slots in 32 different blocks of 8 consecutive slots. `lengths`: the first row of every micro-batch has 128 cached positions.
All inputs are finite; a program needn't handle non-finite values.
Results may differ from a plain program's by a relative error of at most 0.012.
Values may be sent and summed in bfloat16 or wider, within the bound.
A program may use at most 128 MiB of HBM per device.

v0:
```python
import math

import jax
import jax.numpy as jnp
from jax import lax
from jax.sharding import PartitionSpec as P

HEAD_WIDTH = 128


NORM_EPS = 1e-05
ADAPTER_SCALE = 2.0
BEST_PRECISION = lax.Precision.HIGHEST


def passed_along(block, axis, distance):
    devices = range(lax.axis_size(axis))
    route = [(i - distance, i) for i in devices if i - distance in devices]
    return lax.ppermute(block, axis, route)


def attend(queries, keyvals, cache_tick, own_lengths):
    row_count = queries.shape[0]
    kv_width = keyvals.shape[2]
    kv_count = kv_width // HEAD_WIDTH
    group_size = queries.shape[1] // kv_width
    context = cache_tick.shape[1]
    query_heads = queries.reshape(row_count, kv_count, group_size, HEAD_WIDTH)
    key_rows = cache_tick[:, :, 0, :].reshape(row_count, context, kv_count, HEAD_WIDTH)
    value_rows = cache_tick[:, :, 1, :].reshape(row_count, context, kv_count, HEAD_WIDTH)
    new_key = keyvals[:, 0, :].reshape(row_count, kv_count, HEAD_WIDTH)
    new_value = keyvals[:, 1, :].reshape(row_count, kv_count, HEAD_WIDTH)
    inv_scale = 1.0 / math.sqrt(HEAD_WIDTH)
    scores = (
        jnp.einsum("rkgd,rlkd->rkgl", query_heads, key_rows, preferred_element_type=jnp.float32)
        * inv_scale
    )
    own_score = (
        jnp.einsum("rkgd,rkd->rkg", query_heads, new_key, preferred_element_type=jnp.float32)
        * inv_scale
    )
    live_mask = jnp.arange(context, dtype=jnp.int32)[None, :] < own_lengths[:, None]
    weights = jnp.where(live_mask[:, None, None, :], jnp.exp(scores), 0.0)
    own_weight = jnp.exp(own_score)
    denominator = jnp.sum(weights, axis=3) + own_weight
    numerator = jnp.einsum(
        "rkgl,rlkd->rkgd",
        weights.astype(jnp.bfloat16),
        value_rows,
        preferred_element_type=jnp.float32,
    )
    numerator = numerator + jnp.einsum(
        "rkg,rkd->rkgd",
        own_weight.astype(jnp.bfloat16),
        new_value,
        preferred_element_type=jnp.float32,
    )
    return (numerator / denominator[..., None]).astype(jnp.bfloat16).reshape(row_count, -1)


def slot_lists(adapters_per_batch, adapter_slot_table):
    catalog = jnp.arange(adapter_slot_table.shape[0], dtype=jnp.int32)
    wanted = jnp.concatenate([adapters_per_batch[1:], adapters_per_batch[:-1]], axis=1)
    matches = wanted[:, :, None] == catalog[None, None, :]
    return jnp.sum(jnp.where(matches, adapter_slot_table[None, None, :], 0), axis=2)


def pack_panels(panels, all_lists, holder, per_owner, peers_per_segment, capacity):
    group_size = all_lists.shape[0] * peers_per_segment
    peer_ids = jnp.arange(group_size, dtype=jnp.int32)
    layer_of = peer_ids // peers_per_segment
    wanted = all_lists[layer_of]
    owned_mask = wanted // per_owner == holder
    slot_rank = jnp.cumsum(owned_mask.astype(jnp.int32), axis=1) - 1
    local_rows = wanted % per_owner
    slot_ids = jnp.arange(capacity, dtype=jnp.int32)
    matched = owned_mask[:, :, None] & (slot_rank[:, :, None] == slot_ids[None, None, :])
    index_rows = jnp.sum(jnp.where(matched, local_rows[:, :, None], 0), axis=1)
    filled = jnp.any(matched, axis=1)
    picked = panels[index_rows, layer_of[:, None]]
    return jnp.where(filled[:, :, None, None], picked, jnp.zeros_like(picked))


def unpack_panels(received, wanted, per_owner, capacity):
    owner_of = wanted // per_owner
    entries = wanted.shape[0]
    order_ids = jnp.arange(entries, dtype=jnp.int32)
    before = (owner_of[:, None] == owner_of[None, :]) & (order_ids[:, None] > order_ids[None, :])
    slot_rank = jnp.sum(before.astype(jnp.int32), axis=1)
    flattened = received.reshape((-1,) + received.shape[2:])
    return flattened[owner_of * capacity + slot_rank]


def run_layer(
    hidden,
    tick_index,
    batch_index,
    panels_a,
    panels_b,
    gain_row,
    query_weight,
    keyval_weight,
    out_weight,
    cache_local,
    lengths,
    adapter_of_row,
    pool_index,
    tensor_index,
    pool_count,
    tensor_count,
):
    row_count = hidden.shape[0]
    part_rows = row_count // pool_count
    model_width = hidden.shape[1] * pool_count
    expanded_rows = hidden.astype(jnp.float32)
    square_sum = lax.psum(jnp.sum(expanded_rows * expanded_rows, axis=1), "pool")
    normed = (
        expanded_rows * lax.rsqrt(square_sum / model_width + NORM_EPS)[:, None] * gain_row[None, :]
    ).astype(jnp.bfloat16)
    queries = jnp.dot(normed, query_weight, preferred_element_type=jnp.float32)
    keyvals = jnp.einsum("rd,dke->rke", normed, keyval_weight, preferred_element_type=jnp.float32)
    queries, keyvals = (
        lax.psum_scatter(queries, "pool", scatter_dimension=0, tiled=True),
        lax.psum_scatter(keyvals, "pool", scatter_dimension=0, tiled=True),
    )
    queries = queries.astype(jnp.bfloat16)
    keyvals = keyvals.astype(jnp.bfloat16)
    batch_lengths = lax.dynamic_index_in_dim(lengths, batch_index, 0, keepdims=False)
    own_lengths = lax.dynamic_slice_in_dim(batch_lengths, pool_index * part_rows, part_rows)
    attended = attend(queries, keyvals, cache_local[tick_index], own_lengths)
    batch_ids = lax.dynamic_index_in_dim(adapter_of_row, batch_index, 0, keepdims=False)
    act_count = panels_a.shape[0]
    rank_width = panels_a.shape[1]
    up_flattened = panels_b.reshape(act_count * rank_width, -1).astype(jnp.float32)
    adapter_ids = jnp.arange(act_count, dtype=jnp.int32)
    block_rows = lax.all_gather(attended, "pool", axis=0, tiled=True)
    block_count = block_rows.shape[0]
    base_part = jnp.dot(block_rows, out_weight, preferred_element_type=jnp.float32)
    chosen = batch_ids[:, None] == adapter_ids[None, :]
    down_part = jnp.einsum("nq,arq->nar", block_rows, panels_a, preferred_element_type=jnp.float32)
    low_rank = jnp.where(chosen[:, :, None], down_part, 0.0).reshape(
        block_count, act_count * rank_width
    )
    gathered = (base_part, low_rank)
    combined, low_part = gathered
    narrow_sum = lax.psum(low_part, "tensor")
    combined_output = lax.psum(combined, "tensor")
    adapter_update = combined_output + ADAPTER_SCALE * jnp.dot(
        narrow_sum, up_flattened, precision=BEST_PRECISION
    )
    return (expanded_rows + adapter_update).astype(jnp.bfloat16)


def on_device(
    hidden_input,
    fresh,
    gain,
    query_matrix,
    keyval_matrix,
    output_weight,
    cache,
    lengths,
    adapter_of_row,
    adapters_per_batch,
    adapter_slot_table,
    adapter_down,
    adapter_up,
):
    section_index = lax.axis_index("section")
    tensor_index = lax.axis_index("tensor")
    pool_index = lax.axis_index("pool")
    section_count = lax.axis_size("section")
    tensor_count = lax.axis_size("tensor")
    pool_count = lax.axis_size("pool")
    act_count = adapters_per_batch.shape[1]
    all_lists = slot_lists(adapters_per_batch, adapter_slot_table)
    my_list = lax.dynamic_index_in_dim(all_lists, section_index, 0, keepdims=False)
    down_owners = section_count * pool_count
    up_owners = section_count * tensor_count
    down_capacity = 2 * max(1, act_count // down_owners)
    up_capacity = 2 * max(1, act_count // up_owners)
    down_by_slot = adapter_down.shape[0]
    up_by_slot = adapter_up.shape[0]
    send_down = pack_panels(
        adapter_down,
        all_lists,
        section_index * pool_count + pool_index,
        down_by_slot,
        pool_count,
        down_capacity,
    )
    got_down = lax.all_to_all(
        send_down, ("section", "pool"), split_axis=0, concat_axis=0, tiled=True
    )
    panels_down = unpack_panels(got_down, my_list, down_by_slot, down_capacity)
    send_up = pack_panels(
        adapter_up,
        all_lists,
        section_index * tensor_count + tensor_index,
        up_by_slot,
        tensor_count,
        up_capacity,
    )
    got_up = lax.all_to_all(send_up, ("section", "tensor"), split_axis=0, concat_axis=0, tiled=True)
    panels_up = unpack_panels(got_up, my_list, up_by_slot, up_capacity)
    weights_here = (
        gain[0],
        query_matrix[0],
        keyval_matrix[0],
        output_weight[0],
        cache[0],
        lengths,
        adapter_of_row,
        pool_index,
        tensor_index,
        pool_count,
        tensor_count,
    )
    row_count = hidden_input.shape[1]
    piece_rows = row_count // tensor_count
    first_result = run_layer(
        hidden_input[0],
        0,
        section_index + 1,
        panels_down[:act_count],
        panels_up[:act_count],
        *weights_here
    )
    moved = passed_along(first_result, "section", 1)
    first_rows = lax.dynamic_slice_in_dim(first_result, tensor_index * piece_rows, piece_rows)
    incoming = jnp.where(section_index == 0, fresh, moved)
    second_result = run_layer(
        incoming, 1, section_index, panels_down[act_count:], panels_up[act_count:], *weights_here
    )
    second_rows = lax.dynamic_slice_in_dim(second_result, tensor_index * piece_rows, piece_rows)
    return (first_rows[None], second_rows[None])


def solution(mesh):
    return jax.shard_map(
        on_device,
        mesh=mesh,
        in_specs=(
            P("section", None, "pool"),
            P(None, "pool"),
            P("section", "pool"),
            P("section", "pool", "tensor"),
            P("section", "pool", None, "tensor"),
            P("section", "tensor", "pool"),
            P("section", None, "pool", None, None, "tensor"),
            P(),
            P(),
            P(),
            P(),
            P(("section", "pool"), None, None, "tensor"),
            P(("section", "tensor"), None, None, "pool"),
        ),
        out_specs=(P("section", "tensor", "pool"), P("section", "tensor", "pool")),
        check_vma=False,
    )
```

profile of v0, /device:TPU:1, one launch (start us, length us, event | category | flops | bytes accessed | tf_op | source)
XLA Modules:
  0.0 690.2 jit_solution(10896300505061564910)
XLA Ops:
  8.6 35.5 %psum.42 = f32[512]{0:T(512)S(1)} all-reduce(f32[512]{0:T(512)S(1)} %fusion.36), channel_id=1, replica_groups=mesh['section'=2,'tensor'=4,'pool'=16] {'pool'}, use_global_device_ids=true, to_apply=%region_1.2 | all-reduce | flops 512 | bytes 4096 | tf_op jit(solution)/shard_map/psum | solution.py:116
  44.2 2.8 fusion.41
  47.0 3.2 fusion.12
  52.6 2.8 gather_fusion.1
  55.4 4.5 broadcast_select_fusion
  59.9 12.5 %all-to-all-start = ((bf16[32,2,16,2048]{3,2,1,0:T(8,128)(2,1)}), bf16[32,2,16,2048]{3,2,1,0:T(8,128)(2,1)}, u32[]{:S(2)}, u32[]{:S(2)}) async-start(bf16[32,2,16,2048]{3,2,1,0:T(8,128)(2,1)} %broadcast_select_fusion), calls=%async_computation.2 | async-start | bytes 8388608 | tf_op jit(solution)/shard_map/all_to_all | solution.py:192
  72.4 8.5 %fusion.91 = (bf16[1,1,32,128,2,256]{5,4,3,2,1,0:T(2,128)(2,1)}, bf16[1,1,32,128,2,256]{5,4,3,2,1,0:T(2,128)(2,1)}) fusion(bf16[1,2,32,128,2,256]{5,4,3,2,1,0:T(2,128)(2,1)} %param.19), kind=kLoop, calls=%fused_computation.197 | loop fusion | bytes 16777216 | tf_op jit(solution)/shard_map/slice | solution.py:130
  80.9 11.1 %copy.53 = bf16[1,1,32,128,2,256]{3,5,2,4,1,0:T(8,128)(2,1)} copy(bf16[1,1,32,128,2,256]{5,4,3,2,1,0:T(2,128)(2,1)} %get-tuple-element.15) | data formatting | bytes 8388608
  92.9 4.7 fusion.94
  97.6 54.8 %reduce-scatter.7.cloned.1.call-done = f32[32,2,256]{2,0,1:T(8,128)} async-done(((f32[512,2,256]{2,0,1:T(8,128)}), f32[32,2,256]{2,0,1:T(8,128)}) %reduce-scatter.7.cloned.1.call-update) | async-done | bytes 65552 | tf_op jit(solution)/shard_map/reduce_scatter | solution.py:124
  153.2 79.8 %reduce-scatter.5.cloned.1.call-done = f32[32,2048]{1,0:T(8,128)} async-done(((f32[512,2048]{1,0:T(8,128)}), f32[32,2048]{1,0:T(8,128)}) %reduce-scatter.5.cloned.1.call-update) | async-done | bytes 262160 | tf_op jit(solution)/shard_map/reduce_scatter | solution.py:123
  240.0 5.0 gather_fusion.2
  245.0 4.8 fusion.93
  249.8 34.2 %all-gather.3.cloned.1.call-done = bf16[512,2048]{1,0:T(8,128)(2,1)} async-done(((bf16[32,2048]{1,0:T(8,128)(2,1)}), bf16[512,2048]{1,0:T(8,128)(2,1)}) %all-gather.3.cloned.1.call-update) | async-done | bytes 2097168 | tf_op jit(solution)/shard_map/all_gather | solution.py:136
  284.0 3.9 fusion.18
  295.5 6.0 all-to-all-start.1
  301.5 21.5 %all-to-all-done.1 = bf16[8,8,16,512]{3,2,1,0:T(8,128)(2,1)S(1)} async-done(((bf16[8,8,16,512]{3,2,1,0:T(8,128)(2,1)}), bf16[8,8,16,512]{3,2,1,0:T(8,128)(2,1)S(1)}, u32[]{:S(2)}, u32[]{:S(2)}) %all-to-all-start.1) | async-done | bytes 1048608 | tf_op jit(solution)/shard_map/all_to_all | solution.py:204
  324.0 3.0 gather_fusion.5
  329.0 33.3 %all-reduce.7.cloned.1.call-done = (f32[512,512]{1,0:T(8,128)}, f32[512,512]{0,1:T(8,128)}) async-done(((f32[512,512]{1,0:T(8,128)}, f32[512,512]{0,1:T(8,128)}), (f32[512,512]{1,0:T(8,128)}, f32[512,512]{0,1:T(8,128)})) %all-reduce.7.cloned.1.call-update) | async-done | bytes 2097168 | tf_op jit(solution)/shard_map/psum | solution.py:147
  362.3 3.6 fusion.17
  367.2 2.8 collective-permute-done
  372.3 33.4 %psum.45 = f32[512]{0:T(512)S(1)} all-reduce(f32[512]{0:T(512)S(1)} %multiply_reduce_fusion), channel_id=1, replica_groups=mesh['section'=2,'tensor'=4,'pool'=16] {'pool'}, use_global_device_ids=true, to_apply=%region_17.18 | all-reduce | flops 512 | bytes 4096 | tf_op jit(solution)/shard_map/psum | solution.py:116
  405.7 2.5 fusion.39
  408.3 3.3 fusion.10
  411.6 11.1 %copy.55 = bf16[1,1,32,128,2,256]{3,5,2,4,1,0:T(8,128)(2,1)} copy(bf16[1,1,32,128,2,256]{5,4,3,2,1,0:T(2,128)(2,1)} %get-tuple-element.14) | data formatting | bytes 8388608
  422.7 4.7 fusion.92
  427.4 53.8 %reduce-scatter.11.cloned.1.call-done = f32[32,2,256]{2,0,1:T(8,128)} async-done(((f32[512,2,256]{2,0,1:T(8,128)}), f32[32,2,256]{2,0,1:T(8,128)}) %reduce-scatter.11.cloned.1.call-update) | async-done | bytes 65552 | tf_op jit(solution)/shard_map/reduce_scatter | solution.py:124
  482.1 79.3 %reduce-scatter.9.cloned.1.call-done = f32[32,2048]{1,0:T(8,128)} async-done(((f32[512,2048]{1,0:T(8,128)}), f32[32,2048]{1,0:T(8,128)}) %reduce-scatter.9.cloned.1.call-update) | async-done | bytes 262160 | tf_op jit(solution)/shard_map/reduce_scatter | solution.py:123
  562.7 2.4 fusion.98
  567.2 45.2 %all-gather.5.cloned.1.call-done = bf16[512,2048]{1,0:T(8,128)(2,1)} async-done(((bf16[32,2048]{1,0:T(8,128)(2,1)}), bf16[512,2048]{1,0:T(8,128)(2,1)}) %all-gather.5.cloned.1.call-update) | async-done | bytes 2097168 | tf_op jit(solution)/shard_map/all_gather | solution.py:136
  612.3 3.9 fusion.23
  621.7 57.7 %all-reduce.5.cloned.1.call-done = (f32[512,512]{0,1:T(8,128)}, f32[512,512]{1,0:T(8,128)}) async-done(((f32[512,512]{0,1:T(8,128)}, f32[512,512]{1,0:T(8,128)}), (f32[512,512]{0,1:T(8,128)}, f32[512,512]{1,0:T(8,128)})) %all-reduce.5.cloned.1.call-update) | async-done | bytes 2097168 | tf_op jit(solution)/shard_map/psum | solution.py:146
  (123 shorter events, 40.4 us)
Async XLA Ops:
  7.2 39.8 %copy-start = (bf16[1,512,2048]{2,1,0:T(8,128)(2,1)S(1)}, bf16[1,512,2048]{2,1,0:T(8,128)(2,1)}, u32[]{:S(2)}) copy-start(bf16[1,512,2048]{2,1,0:T(8,128)(2,1)} %param.16) | copy-start | bytes 6291460
  7.2 39.8 %copy-start.2 = (bf16[1,512,512]{2,1,0:T(8,128)(2,1)S(1)}, bf16[1,512,512]{2,1,0:T(8,128)(2,1)}, u32[]{:S(2)}) copy-start(bf16[1,512,512]{2,1,0:T(8,128)(2,1)} %param.13) | copy-start | bytes 1572868
  7.2 39.8 %copy-start.7 = (f32[1,512]{1,0:T(1,128)S(1)}, f32[1,512]{1,0:T(1,128)}, u32[]{:S(2)}) copy-start(f32[1,512]{1,0:T(1,128)} %param.15) | copy-start | bytes 6148
  7.2 145.1 %reduce-scatter.7.cloned.1.call-start = ((), (), s32[]{:S(2)}) async-start(), calls=%async_computation.7 | async-start | bytes 1114112 | tf_op jit(solution)/shard_map/reduce_scatter | solution.py:124
  47.0 186.1 %reduce-scatter.5.cloned.1.call-start = ((), (), s32[]{:S(2)}) async-start(), calls=%async_computation.6 | async-start | bytes 4456448 | tf_op jit(solution)/shard_map/reduce_scatter | solution.py:123
  50.3 0.7 copy-start.9
  50.3 0.8 copy-start.10
  50.3 2.4 copy-start.1
  59.9 180.1 %all-to-all-start = ((bf16[32,2,16,2048]{3,2,1,0:T(8,128)(2,1)}), bf16[32,2,16,2048]{3,2,1,0:T(8,128)(2,1)}, u32[]{:S(2)}, u32[]{:S(2)}) async-start(bf16[32,2,16,2048]{3,2,1,0:T(8,128)(2,1)} %broadcast_select_fusion), calls=%async_computation.2 | async-start | bytes 8388608 | tf_op jit(solution)/shard_map/all_to_all | solution.py:192
  72.4 211.6 %all-gather.3.cloned.1.call-start = ((), (), s32[]{:S(2)}) async-start(), calls=%async_computation.8 | async-start | bytes 2228224 | tf_op jit(solution)/shard_map/all_gather | solution.py:136
  233.1 3.8 copy-start.6
  236.8 3.1 copy-start.8
  238.8 123.5 %all-reduce.7.cloned.1.call-start = ((), (), s32[]{:S(2)}) async-start(), calls=%async_computation.13 | async-start | bytes 4194304 | tf_op jit(solution)/shard_map/psum | solution.py:147
  284.0 5.5 copy-start.13
  287.9 1.6 copy-start.11
  295.5 27.5 %all-to-all-start.1 = ((bf16[8,8,16,512]{3,2,1,0:T(8,128)(2,1)}), bf16[8,8,16,512]{3,2,1,0:T(8,128)(2,1)S(1)}, u32[]{:S(2)}, u32[]{:S(2)}) async-start(bf16[8,8,16,512]{3,2,1,0:T(8,128)(2,1)} %broadcast_select_fusion.1), calls=%async_computation.3 | async-start | bytes 2097152 | tf_op jit(solution)/shard_map/all_to_all | solution.py:204
  301.5 179.7 %reduce-scatter.11.cloned.1.call-start = ((), (), s32[]{:S(2)}) async-start(), calls=%async_computation.10 | async-start | bytes 1114112 | tf_op jit(solution)/shard_map/reduce_scatter | solution.py:124
  323.0 1.0 copy-start.4
  324.0 38.3 %copy-start.3 = (bf16[1,512,512]{2,1,0:T(8,128)(2,1)S(1)}, bf16[1,512,512]{2,1,0:T(8,128)(2,1)}, u32[]{:S(2)}) copy-start(bf16[1,512,512]{2,1,0:T(8,128)(2,1)} %param.13) | copy-start | bytes 1572868
  365.9 4.1 collective-permute-start
  408.2 153.2 %reduce-scatter.9.cloned.1.call-start = ((), (), s32[]{:S(2)}) async-start(), calls=%async_computation.9 | async-start | bytes 4456448 | tf_op jit(solution)/shard_map/reduce_scatter | solution.py:123
  411.6 200.7 %all-gather.5.cloned.1.call-start = ((), (), s32[]{:S(2)}) async-start(), calls=%async_computation.11 | async-start | bytes 2228224 | tf_op jit(solution)/shard_map/all_gather | solution.py:136
  561.4 3.8 copy-start.5
  567.1 112.2 %all-reduce.5.cloned.1.call-start = ((), (), s32[]{:S(2)}) async-start(), calls=%async_computation.12 | async-start | bytes 4194304 | tf_op jit(solution)/shard_map/psum | solution.py:146
  612.3 5.5 copy-start.14
  616.2 1.6 copy-start.12
Sparse Core Ops, SparseCore 0:
  47.1 105.2 reduce-scatter.6
  156.0 76.9 reduce-scatter.4
  238.9 45.0 all-gather.2
  291.9 70.3 all-reduce.6
  408.3 72.8 reduce-scatter.10
  484.4 76.9 reduce-scatter.8
  567.2 45.0 all-gather.4
  620.2 59.0 all-reduce.4
where the time goes:
time: 692 us; the launch traced here: 690 us
  waiting for transfers between devices  462 us (67%)
  local copies, waits for them, and re-layouts  69.8 us (10%)
  blocking collectives  68.9 us (10%)
  matrix products  37.4 us (5%)
  starting transfers between devices  20 us (3%)
  other arithmetic  17.1 us (2%)
  between operations  14.5 us (2%)
    reduce_scatter x2, waiting for transfers between devices, run_layer(): lax.psum_scatter(queries, 'pool', scatter_dimension=0, tiled=True)  159 us
    reduce_scatter x2, waiting for transfers between devices, run_layer(): lax.psum_scatter(keyvals, 'pool', scatter_dimension=0, tiled=True)  109 us
    all_gather x2, waiting for transfers between devices, run_layer(): block_rows = lax.all_gather(attended, 'pool', axis=0, tiled=True)  79.4 us
    psum x2, blocking collectives, run_layer(): lax.psum(jnp.sum(expanded_rows * expanded_rows, axis=1), 'pool')  68.9 us
    psum x1, waiting for transfers between devices, run_layer(): narrow_sum = lax.psum(low_part, 'tensor')  57.7 us
    psum x1, waiting for transfers between devices, run_layer(): combined_output = lax.psum(combined, 'tensor')  33.3 us
    unnamed x36, local copies, waits for them, and re-layouts  25.2 us
    all_to_all x1, waiting for transfers between devices, on_device(): lax.all_to_all(send_up, ('section', 'tensor'), split_axis=0, concat_axis=...  21.5 us
  transfers between devices with their start and end apart: 11, of which 10 were waited for; matrix products, arithmetic and copies ran while one was open for 12% of the time, Pallas kernels for 0%

commit v1 on v0

v1 whole, which is shorter than its diff:
```python
import functools
import math

import jax
import jax.numpy as jnp
from jax import lax
from jax.experimental import pallas as pl
from jax.experimental.pallas import tpu as pltpu
from jax.sharding import PartitionSpec as P

NORM_EPS = 1e-05
ADAPTER_SCALE = 2.0
MESH = pl.DeviceIdType.MESH
F32 = jnp.float32
BF16 = jnp.bfloat16

RING = 4
ROWS = 512
FEAT = 512
MODEL = 8192
QCOLS = 2048
KVCOLS = 256
HEADS = 16
HEAD = 128
CTX = 128
CW = QCOLS + 2 * KVCOLS + 128
OWN_ROWS = 32
HALF_ROWS = 16
RANK = 16
N_SEM = 224


def dot(a, b):
    return jnp.dot(a, b, preferred_element_type=F32)


def kernel(
    hidden_hbm,
    fresh_hbm,
    gain_ref,
    wq_hbm,
    wkv_hbm,
    wo_hbm,
    cache_hbm,
    len_ref,
    aor_ref,
    apb_ref,
    table_ref,
    down_hbm,
    up_hbm,
    first_ref,
    second_ref,
    wall,
    kvraw,
    wo,
    dn,
    upv,
    sel,
    upbuf,
    kbuf,
    cbuf,
    fwd1,
    fin1,
    c2,
    fin2,
    agbuf,
    ob,
    finx,
    xin,
    ubuf,
    rslot,
    qs,
    kns,
    vns,
    att,
    lrown,
    lrx,
    lrp,
    ssem,
    rsem,
    lsem,
    psend,
    precv,
    turn,
):
    s = lax.axis_index("section")
    t = lax.axis_index("tensor")
    p = lax.axis_index("pool")
    z = p // RING
    y = p % RING
    o = 1 - s
    outs = (first_ref, second_ref)

    def ring(i, d):
        return lax.rem(i + d + 2 * RING, RING)

    def at_z(j):
        return {"pool": j * RING + y}

    def at_y(j):
        return {"pool": z * RING + j}

    def at_x(j):
        return {"tensor": j}

    started = []
    used = [0]

    def remote(src, dst, dev):
        n = used[0]
        used[0] += 1
        assert n < N_SEM
        return pltpu.make_async_remote_copy(
            src_ref=src,
            dst_ref=dst,
            send_sem=ssem.at[n],
            recv_sem=rsem.at[n],
            device_id=dev,
            device_id_type=MESH,
        )

    def tracked(src, dst, dev):
        c = remote(src, dst, dev)
        started.append(c)
        return c

    def send(src, dst, dev):
        c = tracked(src, dst, dev)
        c.start()
        return c

    kvflat = wkv_hbm.reshape(2 * FEAT, KVCOLS)
    cflat = cache_hbm.reshape(2, OWN_ROWS, 2 * CTX, KVCOLS)
    load_x0 = pltpu.make_async_copy(hidden_hbm.at[0], xin.at[0], lsem.at[0])
    load_kv = pltpu.make_async_copy(kvflat, kvraw, lsem.at[1])
    load_wq = pltpu.make_async_copy(wq_hbm.at[0], wall.at[:, 0:QCOLS], lsem.at[2])
    load_up = pltpu.make_async_copy(up_hbm, upv, lsem.at[3])
    load_dn = pltpu.make_async_copy(down_hbm.at[:, s], dn.at[0], lsem.at[4])
    load_c = [
        pltpu.make_async_copy(cflat.at[k], kbuf.at[k], lsem.at[5 + k]) for k in range(2)
    ]
    load_wo = pltpu.make_async_copy(wo_hbm.at[0], wo.at[:, 0:FEAT], lsem.at[7])
    load_x0.start()
    load_kv.start()
    load_wq.start()
    load_fresh = pltpu.make_async_copy(fresh_hbm, xin.at[1], lsem.at[8])

    barrier = pltpu.get_barrier_semaphore()

    def greet(d, _):
        pl.semaphore_signal(
            barrier, inc=1, device_id={"pool": lax.rem(p + d, 16)}, device_id_type=MESH
        )
        return _

    lax.fori_loop(1, 16, greet, 0)
    for d in range(1, RING):
        pl.semaphore_signal(
            barrier, inc=1, device_id={"tensor": ring(t, d)}, device_id_type=MESH
        )
    for d in range(RING):
        pl.semaphore_signal(
            barrier,
            inc=1,
            device_id={"section": o, "tensor": ring(t, d)},
            device_id_type=MESH,
        )

    load_kv.wait()
    pick_r = lax.broadcasted_iota(jnp.int32, (128, 256), 0)
    pick_c = lax.broadcasted_iota(jnp.int32, (128, 256), 1)
    for b in range(4):
        block = kvraw[b * 256 : (b + 1) * 256, :]
        for n in range(2):
            pick = jnp.where(pick_c == 2 * pick_r + n, 1.0, 0.0).astype(BF16)
            wall[
                b * 128 : (b + 1) * 128,
                QCOLS + n * KVCOLS : QCOLS + (n + 1) * KVCOLS,
            ] = dot(pick, block).astype(BF16)

    def project(k):
        for r in range(RING):
            rows = slice(r * 128, (r + 1) * 128)
            xf = xin[k, rows, :].astype(F32)
            ubuf[rows, :] = (xf * gain_ref[...]).astype(BF16)
            ss = jnp.sum(xf * xf, axis=1, keepdims=True)
            cbuf[k, r, :, :, :, QCOLS + 2 * KVCOLS : CW] = (
                jnp.broadcast_to(ss, (128, 128)).astype(BF16).reshape(4, 2, HALF_ROWS, 128)
            )

        def tile(n, _):
            cols = pl.ds(pl.multiple_of(n * 512, 512), 512)
            part = dot(ubuf[...], wall[:, cols])
            cbuf[k, :, :, :, :, cols] = part.astype(BF16).reshape(4, 4, 2, HALF_ROWS, 512)
            return _

        lax.fori_loop(0, (QCOLS + 2 * KVCOLS) // 512, tile, 0)

    class RingSum:
        def __init__(self, i, dev, src, fwd, fin):
            right, left = ring(i, 1), ring(i, -1)
            self.add0, self.fwd0 = src(right, 0), fwd(0)
            self.add1, self.fwd1 = src(left, 1), fwd(1)
            self.f0 = tracked(src(ring(i, 2), 0), fwd(0), dev(right))
            self.f1 = tracked(src(ring(i, 2), 1), fwd(1), dev(left))
            self.a0 = tracked(src(right, 1), fin(0, 1), dev(right))
            self.a1 = tracked(src(left, 0), fin(1, 0), dev(left))
            self.b0 = tracked(self.add0, fin(0, 0), dev(right))
            self.b1 = tracked(self.add1, fin(1, 1), dev(left))

        def begin(self):
            for c in (self.f0, self.f1, self.a0, self.a1):
                c.start()

        def middle(self):
            self.f0.wait_recv()
            v, w = self.add0, self.fwd0
            v[...] = (v[...].astype(F32) + w[...].astype(F32)).astype(BF16)
            self.b0.start()
            self.f1.wait_recv()
            v, w = self.add1, self.fwd1
            v[...] = (v[...].astype(F32) + w[...].astype(F32)).astype(BF16)
            self.b1.start()

        def end(self):
            for c in (self.a0, self.a1, self.b0, self.b1):
                c.wait_recv()

    class RingGather:
        def __init__(self, i, dev, block):
            right, left = ring(i, 1), ring(i, -1)
            self.r0 = tracked(block(i, 0), block(i, 0), dev(right))
            self.l1 = tracked(block(i, 1), block(i, 1), dev(left))
            self.r1 = tracked(block(i, 1), block(i, 1), dev(right))
            self.l0 = tracked(block(i, 0), block(i, 0), dev(left))
            self.f0 = tracked(block(left, 0), block(left, 0), dev(right))
            self.f1 = tracked(block(right, 1), block(right, 1), dev(left))

        def begin(self):
            for c in (self.r0, self.l1, self.r1, self.l0):
                c.start()

        def middle(self):
            self.r0.wait_recv()
            self.f0.start()
            self.l1.wait_recv()
            self.f1.start()

        def end(self):
            for c in (self.r1, self.l0, self.f0, self.f1):
                c.wait_recv()

    class DirectSum:
        def __init__(self, i, dev, src, fin):
            self.copies = [
                tracked(src(ring(i, d)), fin(d - 1), dev(ring(i, d))) for d in (2, 1, 3)
            ]

        def begin(self):
            for c in self.copies:
                c.start()

        def end(self):
            for c in self.copies:
                c.wait_recv()

    class DirectGather:
        def __init__(self, i, dev, block):
            self.copies = [
                tracked(block(i), block(i), dev(ring(i, d))) for d in (2, 1, 3)
            ]

        def begin(self):
            for c in self.copies:
                c.start()

        def end(self):
            for c in self.copies:
                c.wait_recv()

    def pool_rings(k):
        first = [
            RingSum(
                z,
                at_z,
                lambda j, hf: cbuf.at[k, j, 2 * hf : 2 * hf + 2, 0],
                lambda d: fwd1.at[k, 0, d],
                lambda d, hf: fin1.at[k, 0, d, 2 * hf : 2 * hf + 2],
            ),
            RingSum(
                y,
                at_y,
                lambda j, hf: cbuf.at[k, 2 * hf : 2 * hf + 2, j, 1],
                lambda d: fwd1.at[k, 1, d],
                lambda d, hf: fin1.at[k, 1, d, 2 * hf : 2 * hf + 2],
            ),
        ]
        second = [
            DirectSum(
                (y, z)[h],
                (at_y, at_z)[h],
                lambda j, h=h: c2.at[k, h, j],
                lambda n, h=h: fin2.at[k, h, n],
            )
            for h in range(2)
        ]
        return first, second

    def sum_begin(k):
        for r in rings[k][0]:
            r.begin()

    def sum_middle(k):
        for r in rings[k][0]:
            r.middle()

    def sum_second(k):
        first, second = rings[k]
        for h in range(2):
            first[h].end()
            for b in range(RING):
                mine = cbuf[k, z, b, 0] if h == 0 else cbuf[k, b, y, 1]
                c2[k, h, b] = (
                    mine.astype(F32)
                    + fin1[k, h, 0, b].astype(F32)
                    + fin1[k, h, 1, b].astype(F32)
                ).astype(BF16)
            second[h].begin()

    def sum_end(k):
        for h in range(2):
            rings[k][1][h].end()
            total = c2[k, h, y if h == 0 else z].astype(F32)
            for n in range(3):
                total = total + fin2[k, h, n].astype(F32)
            rstd = lax.rsqrt(total[:, QCOLS + 2 * KVCOLS :] * (1.0 / MODEL) + NORM_EPS)

            def part(n):
                return (total[:, n * HEAD : (n + 1) * HEAD] * rstd).astype(BF16).astype(F32)

            keys = [part(HEADS + g) for g in range(2)]
            values = [part(HEADS + 2 + g) for g in range(2)]
            for n in range(HEADS):
                at = pl.ds(h * HALF_ROWS * HEADS + n, HALF_ROWS, stride=HEADS)
                qs[at, :] = part(n)
                kns[at, :] = keys[n // 8]
                vns[at, :] = values[n // 8]

    inv_scale = 1.0 / math.sqrt(HEAD)
    group = 128 // HEADS
    lane = lax.broadcasted_iota(jnp.int32, (1, 128), 1)
    lane_row = lane // HEADS
    low_heads = lane - lane_row * HEADS < 8
    position = lax.broadcasted_iota(jnp.int32, (2 * CTX, 128), 0)
    even = (position & 1) == 0

    def attention(k):
        for i in range(OWN_ROWS // group):
            at = slice(i * 128, (i + 1) * 128)
            q = qs[at, :]
            own = jnp.exp(jnp.sum(q * kns[at, :], axis=1, keepdims=True) * inv_scale)
            qt = q.T
            wide = jnp.concatenate(
                [jnp.where(low_heads, qt, 0.0), jnp.where(low_heads, 0.0, qt)], axis=0
            )
            length = jnp.zeros((1, 128), jnp.int32)
            scores = jnp.zeros((2 * CTX, 128), F32)
            for r in range(group):
                mine = lane_row == r
                scores = scores + dot(
                    kbuf[k, i * group + r], jnp.where(mine, wide, 0.0).astype(BF16)
                )
                length = jnp.where(
                    mine, len_ref[s + 1 - k, p * OWN_ROWS + i * group + r], length
                )
            live = even & (position < 2 * length)
            weights = jnp.where(live, jnp.exp(jnp.where(live, scores, 0.0) * inv_scale), 0.0)
            weights = pltpu.roll(weights, 1, 0).T
            den = jnp.sum(weights, axis=1, keepdims=True) + own
            weights = weights.astype(BF16)
            nums = []
            for r in range(group):
                pv = dot(weights[r * HEADS : (r + 1) * HEADS], kbuf[k, i * group + r])
                nums += [pv[:8, :HEAD], pv[8:, HEAD:]]
            num = jnp.concatenate(nums, axis=0) + own.astype(BF16).astype(F32) * vns[at, :]
            att[at, :] = num / den
        for h in range(2):
            for n in range(HEADS):
                at = pl.ds(h * HALF_ROWS * HEADS + n, HALF_ROWS, stride=HEADS)
                agbuf[k, z, y, h, :, n * HEAD : (n + 1) * HEAD] = att[at, :].astype(BF16)

    def gather_rings(k):
        first = [
            DirectGather(y, at_y, lambda j: agbuf.at[k, z, j, 0]),
            DirectGather(z, at_z, lambda j: agbuf.at[k, j, y, 1]),
        ]
        second = [
            RingGather(z, at_z, lambda j, hf: agbuf.at[k, j, 2 * hf : 2 * hf + 2, 0]),
            RingGather(y, at_y, lambda j, hf: agbuf.at[k, 2 * hf : 2 * hf + 2, j, 1]),
        ]
        return first, second

    def gather_begin(k):
        for r in gathers[k][0]:
            r.begin()

    def gather_second(k):
        first, second = gathers[k]
        for h in range(2):
            first[h].end()
            second[h].begin()

    def gather_end(k):
        second = gathers[k][1]
        for r in second:
            r.middle()
        for r in second:
            r.end()

    def output_products(k):
        for pair in ((2, 1), (3, 0)):
            chunks = [ring(t, d) for d in pair]
            rows = jnp.concatenate([agbuf[k, j].reshape(128, QCOLS) for j in chunks], axis=0)
            both = dot(rows, wo[...])
            for n, j in enumerate(chunks):
                ob[k, j] = both[n * 128 : (n + 1) * 128, :FEAT].astype(BF16)
                down = both[n * 128 : (n + 1) * 128, FEAT:].T
                ids = rslot[pl.ds(k, 1), pl.ds(pl.multiple_of(j * 128, 128), 128)]
                acc = jnp.zeros((RANK, 128), F32)
                for m in range(16):
                    slot = ((s if m < 8 else o) * 16 + p) * 8 + m % 8
                    acc = acc + jnp.where(
                        ids == slot, down[m * RANK : (m + 1) * RANK, :], 0.0
                    )
                lrown[k, j] = acc
            for d in pair:
                if d > 0:
                    lows[k][d - 1].start()
                    tops[k][d - 1].start()

    def output_low(k):
        total = lrown[k, t]
        for d in range(1, RING):
            lows[k][d - 1].wait_recv()
            total = total + lrx[k, ring(t, -d)]
        lrp[k, p] = total.astype(BF16)

        def give(d, _):
            pltpu.make_async_remote_copy(
                src_ref=lrp.at[k, p],
                dst_ref=lrp.at[k, p],
                send_sem=psend.at[k, d],
                recv_sem=precv.at[k, d],
                device_id={"pool": lax.rem(p + d, 16)},
                device_id_type=MESH,
            ).start()
            return _

        lax.fori_loop(1, 16, give, 0)

    def output_delta(k):
        def take(d, _):
            pltpu.make_async_remote_copy(
                src_ref=lrp.at[k, p],
                dst_ref=lrp.at[k, p],
                send_sem=psend.at[k, d],
                recv_sem=precv.at[k, d],
                device_id={"pool": lax.rem(p + d, 16)},
                device_id_type=MESH,
            ).wait()
            return _

        lax.fori_loop(1, 16, take, 0)
        low_rank = lrp[k, 0].astype(F32)
        for n in range(1, 16):
            low_rank = low_rank + lrp[k, n].astype(F32)
        for c in panels[k]:
            c.wait_recv()
        ids = rslot[pl.ds(k, 1), pl.ds(pl.multiple_of(t * 128, 128), 128)]
        block = lax.shift_right_logical(ids, 3)
        wide = jnp.concatenate(
            [jnp.where(block == b, low_rank, 0.0) for b in range(32)], axis=0
        )
        delta = dot(wide.T.astype(BF16), upbuf[k].reshape(512, FEAT))
        row = pl.ds(pl.multiple_of(t * 128, 128), 128)
        total = (
            xin[k, row, :].astype(F32) + ob[k, t].astype(F32) + ADAPTER_SCALE * delta
        )
        for d in range(1, RING):
            tops[k][d - 1].wait_recv()
            total = total + finx[k, d - 1].astype(F32)
        outs[k][0] = total.astype(BF16)

    def slots_and_offsets():
        ids = [aor_ref[pl.ds(s + 1 - k, 1), :] for k in range(2)]
        first_block = (s * RING + t) * 4

        def step(a, carry):
            rows, offs = carry
            slots = [table_ref[apb_ref[c, a]] for c in range(3)]
            new_offs = []
            for c in range(3):
                block = lax.shift_right_logical(slots[c], 3) - first_block
                new_offs += [
                    jnp.where(block == j, slots[c] & 7, offs[4 * c + j]) for j in range(4)
                ]
            new_rows = []
            for k in range(2):
                slot = jnp.where(s == 0, slots[1 - k], slots[2 - k])
                new_rows.append(jnp.where(ids[k] == a, slot, rows[k]))
            return tuple(new_rows), tuple(new_offs)

        rows, offs = lax.fori_loop(
            0,
            32,
            step,
            ((jnp.zeros((1, ROWS), jnp.int32),) * 2, (jnp.int32(0),) * 12),
        )
        for k in range(2):
            rslot[pl.ds(k, 1), :] = rows[k]
        return offs

    def give_panels(offs):
        got = [[], []]
        mine = s * RING + t
        for w in range(2):
            layer = s if w == 0 else o
            for k in range(2):
                for j in range(4):
                    off = jnp.where(layer == 0, offs[4 * (1 - k) + j], offs[4 * (2 - k) + j])
                    sel[w, k, j * RANK : (j + 1) * RANK, :] = upv[8 * j + off, layer]
                if w == 0:
                    upbuf[k, mine] = sel[w, k]
                for d in range(1 if w == 0 else 0, RING):
                    got[k].append(
                        send(
                            sel.at[w, k],
                            upbuf.at[k, mine],
                            {"section": layer, "tensor": ring(t, d)},
                        )
                    )
        return got

    def spread_down():
        for n in range(2):
            for m in range(QCOLS // 128):
                panel = dn[n, :, :, m * 128 : (m + 1) * 128].reshape(8 * RANK, 128)
                wo[m * 128 : (m + 1) * 128, FEAT + n * 128 : FEAT + (n + 1) * 128] = (
                    panel.astype(F32).T.astype(BF16)
                )

    rings = [pool_rings(k) for k in range(2)]
    gathers = [gather_rings(k) for k in range(2)]
    lows = [
        [
            tracked(lrown.at[k, ring(t, d)], lrx.at[k, t], at_x(ring(t, d)))
            for d in range(1, RING)
        ]
        for k in range(2)
    ]
    tops = [
        [
            tracked(ob.at[k, ring(t, d)], finx.at[k, d - 1], at_x(ring(t, d)))
            for d in range(1, RING)
        ]
        for k in range(2)
    ]

    load_x0.wait()
    load_wq.wait()
    load_up.start()
    load_c[0].start()

    @pl.when(s == 0)
    def _():
        load_fresh.start()

    load_wo.start()
    load_dn.start()
    load_c[1].start()
    project(0)
    pl.semaphore_wait(barrier, 22)
    other_down = send(down_hbm.at[:, o], dn.at[1], {"section": o})

    @pl.when(s == 1)
    def _():
        pl.semaphore_wait(turn, 1)

    sum_begin(0)
    offs = slots_and_offsets()
    sum_middle(0)

    @pl.when(s == 0)
    def _():
        load_fresh.wait()
        project(1)

    sum_second(0)
    load_up.wait()
    panels = give_panels(offs)
    sum_end(0)

    @pl.when(s == 0)
    def _():
        pl.semaphore_signal(turn, inc=1, device_id={"section": o}, device_id_type=MESH)

    load_c[0].wait()
    attention(0)
    gather_begin(0)
    load_dn.wait()
    other_down.wait_recv()
    load_wo.wait()
    spread_down()
    gather_second(0)
    gather_end(0)

    row = pl.ds(pl.multiple_of(t * 128, 128), 128)
    relay = [
        remote(first_ref.at[0], xin.at[1, row], {"section": 1, "tensor": ring(t, d)})
        for d in range(RING)
    ]

    @pl.when(s == 1)
    def _():
        for c in relay:
            c.wait_recv()
        project(1)

    sum_begin(1)
    output_products(0)

    @pl.when(s == 1)
    def _():
        sum_middle(1)

    output_low(0)

    @pl.when(s == 1)
    def _():
        sum_second(1)

    output_delta(0)

    @pl.when(s == 0)
    def _():
        for d in (2, 1, 3, 0):
            relay[d].start()
        sum_middle(1)
        sum_second(1)
        for c in relay:
            c.wait_send()

    sum_end(1)
    load_c[1].wait()
    attention(1)
    gather_begin(1)
    gather_second(1)
    gather_end(1)
    output_products(1)
    output_low(1)
    output_delta(1)
    for c in started:
        c.wait_send()


def hand_over(first_in, second_in, first_out, second_out):
    first_out[...] = first_in[...]
    second_out[...] = second_in[...]


def on_device(*args):
    any_space = pl.BlockSpec(memory_space=pl.ANY)
    vmem = pl.BlockSpec(memory_space=pltpu.VMEM)
    smem = pl.BlockSpec(memory_space=pltpu.SMEM)
    out = jax.ShapeDtypeStruct((1, 128, FEAT), BF16)
    v = pltpu.VMEM
    dma = pltpu.SemaphoreType.DMA
    first, second = pl.pallas_call(
        kernel,
        out_shape=(out, out),
        in_specs=[
            any_space,
            any_space,
            vmem,
            any_space,
            any_space,
            any_space,
            any_space,
            smem,
            vmem,
            smem,
            smem,
            any_space,
            any_space,
        ],
        out_specs=(vmem, vmem),
        scratch_shapes=[
            v((FEAT, QCOLS + 2 * KVCOLS), BF16),
            v((2 * FEAT, KVCOLS), BF16),
            v((QCOLS, FEAT + 16 * RANK), BF16),
            v((2, 8, RANK, QCOLS), BF16),
            v((32, 2, RANK, FEAT), BF16),
            v((2, 2, 4 * RANK, FEAT), BF16),
            v((2, 8, 4 * RANK, FEAT), BF16),
            v((2, OWN_ROWS, 2 * CTX, KVCOLS), BF16),
            v((2, RING, RING, 2, HALF_ROWS, CW), BF16),
            v((2, 2, 2, 2, HALF_ROWS, CW), BF16),
            v((2, 2, 2, RING, HALF_ROWS, CW), BF16),
            v((2, 2, RING, HALF_ROWS, CW), BF16),
            v((2, 2, 3, HALF_ROWS, CW), BF16),
            v((2, RING, RING, 2, HALF_ROWS, QCOLS), BF16),
            v((2, RING, 128, FEAT), BF16),
            v((2, 3, 128, FEAT), BF16),
            v((2, ROWS, FEAT), BF16),
            v((ROWS, FEAT), BF16),
            v((8, ROWS), jnp.int32),
            v((OWN_ROWS * HEADS, HEAD), F32),
            v((OWN_ROWS * HEADS, HEAD), F32),
            v((OWN_ROWS * HEADS, HEAD), F32),
            v((OWN_ROWS * HEADS, HEAD), F32),
            v((2, RING, RANK, 128), F32),
            v((2, RING, RANK, 128), F32),
            v((2, 16, RANK, 128), BF16),
            dma((N_SEM,)),
            dma((N_SEM,)),
            dma((9,)),
            dma((2, 16)),
            dma((2, 16)),
            pltpu.SemaphoreType.REGULAR,
        ],
        compiler_params=pltpu.CompilerParams(
            collective_id=0, has_side_effects=True, vmem_limit_bytes=58 * 2**20
        ),
        cost_estimate=pl.CostEstimate(
            flops=8_000_000_000, bytes_accessed=16_000_000, transcendentals=500_000
        ),
    )(*args)
    return pl.pallas_call(
        hand_over,
        out_shape=(out, out),
        in_specs=[vmem, vmem],
        out_specs=(vmem, vmem),
    )(first, second)


def solution(mesh):
    return jax.shard_map(
        on_device,
        mesh=mesh,
        in_specs=(
            P("section", None, "pool"),
            P(None, "pool"),
            P("section", "pool"),
            P("section", "pool", "tensor"),
            P("section", "pool", None, "tensor"),
            P("section", "tensor", "pool"),
            P("section", None, "pool", None, None, "tensor"),
            P(),
            P(),
            P(),
            P(),
            P(("section", "pool"), None, None, "tensor"),
            P(("section", "tensor"), None, None, "pool"),
        ),
        out_specs=(P("section", "tensor", "pool"), P("section", "tensor", "pool")),
        check_vma=False,
    )
```

time: 692 us -> 111 us (0.16)
  waiting for transfers between devices: 462 us -> 0 us
  Pallas kernels: 0 us -> 110 us
  local copies, waits for them, and re-layouts: 69.8 us -> 0 us
  blocking collectives: 68.9 us -> 0 us
  matrix products: 37.4 us -> 0 us
  starting transfers between devices: 20 us -> 0 us
  other arithmetic: 17.1 us -> 0 us
  between operations: 14.5 us -> 0.64 us
    reduce_scatter x4 -> x0, waiting for transfers between devices: 268 us -> none  [the longest x2 159 us: run_layer(): lax.psum_scatter(queries, 'pool', scatter_dimension=0, tiled=True)]
    pallas_call x0 -> x2, Pallas kernels: none -> 110 us  [the longest x1 108 us: on_device(): pl.pallas_call(kernel, out_shape=(out, out), in_specs=[any_space, any_spa...]
    psum x2 -> x0, waiting for transfers between devices: 90.9 us -> none  [the longest x1 57.7 us: run_layer(): narrow_sum = lax.psum(low_part, 'tensor')]
    all_gather x2 -> x0, waiting for transfers between devices: 79.4 us -> none  [run_layer(): block_rows = lax.all_gather(attended, 'pool', axis=0, tiled=True)]
    psum x2 -> x0, blocking collectives: 68.9 us -> none  [run_layer(): lax.psum(jnp.sum(expanded_rows * expanded_rows, axis=1), 'pool')]
    dot_general x16 -> x0, matrix products: 37.4 us -> none  [the longest x2 7.76 us: run_layer(): jnp.einsum('nq,arq->nar', block_rows, panels_a, preferred_element_type=jn...]
    unnamed x36 -> x0, local copies, waits for them, and re-layouts: 25.2 us -> none
    slice x6 -> x0, local copies, waits for them, and re-layouts: 24.8 us -> none  [the longest x2 9.4 us: attend(): cache_tick[:, :, 0, :].reshape(row_count, context, kv_count, HEAD_WIDTH)]
  transfers between devices with their start and end apart: 11 -> 0, of which waited for: 10 -> 0; matrix products, arithmetic and copies ran while one was open for 12% -> 0% of each run, Pallas kernels for 0% -> 0%
where the time goes in v1:
time: 111 us
  Pallas kernels  110 us (99%)
    pallas_call x1, Pallas kernels, on_device(): pl.pallas_call(kernel, out_shape=(out, out), in_specs=[any_space, any_spa...  108 us

profile of v1, /device:TPU:1, one launch (start us, length us, event | category | flops | bytes accessed | tf_op | source)
XLA Modules:
  0.0 110.7 jit_solution(8922802375359026457)
XLA Ops:
  0.6 108.4 %shard_map.140 = (bf16[1,128,512]{2,1,0:T(8,128)(2,1)}, bf16[1,128,512]{2,1,0:T(8,128)(2,1)}) custom-call(bf16[1,512,512]{2,1,0:T(8,128)(2,1)} %hidden_hbm.1, bf16[512,512]{1,0:T(8,128)(2,1)} %fresh_hbm.1, f32[1,512]{1,0:T(1,128)} %gain_ref.1, bf16[1,512,2048]{2,1,0:T(8,128)(2,1)} %wq_hbm.1, bf16[1,512,2,256]{3,2,1,0:T(2,128)(2,1)} %wkv_hbm.1, ...), custom_call_target="tpu_custom_call" | custom-call | flops 8000000000 | bytes 16000000 | tf_op jit(solution)/shard_map/pallas_call | solution.py:678
  109.1 1.7 %shard_map.141 = (bf16[1,128,512]{2,1,0:T(8,128)(2,1)}, bf16[1,128,512]{2,1,0:T(8,128)(2,1)}) custom-call(bf16[1,128,512]{2,1,0:T(8,128)(2,1)} %get-tuple-element.4.first_in, bf16[1,128,512]{2,1,0:T(8,128)(2,1)} %get-tuple-element.5.second_in), custom_call_target="tpu_custom_call" | custom-call | tf_op jit(solution)/shard_map/pallas_call | solution.py:738

commit v2 on v1

--- a/solution.py
+++ b/solution.py
@@ -24,6 +24,8 @@
 HEAD = 128
 CTX = 128
 CW = QCOLS + 2 * KVCOLS + 128
+WIDTHS = (1408, CW - 1408)
+STARTS = (0, 1408)
 OWN_ROWS = 32
 HALF_ROWS = 16
 RANK = 16
@@ -68,7 +70,8 @@
     finx,
     xin,
     ubuf,
-    rslot,
+    half_slot,
+    chunk_slot,
     qs,
     kns,
     vns,
@@ -178,20 +181,19 @@
                 QCOLS + n * KVCOLS : QCOLS + (n + 1) * KVCOLS,
             ] = dot(pick, block).astype(BF16)
 
-    def project(k):
-        for r in range(RING):
-            rows = slice(r * 128, (r + 1) * 128)
-            xf = xin[k, rows, :].astype(F32)
-            ubuf[rows, :] = (xf * gain_ref[...]).astype(BF16)
-            ss = jnp.sum(xf * xf, axis=1, keepdims=True)
-            cbuf[k, r, :, :, :, QCOLS + 2 * KVCOLS : CW] = (
-                jnp.broadcast_to(ss, (128, 128)).astype(BF16).reshape(4, 2, HALF_ROWS, 128)
-            )
+    def project(k, m):
+        base = [q * OWN_ROWS + m * HALF_ROWS for q in range(16)]
+        xf = jnp.concatenate([xin[k, b : b + HALF_ROWS, :] for b in base], axis=0).astype(F32)
+        ubuf[...] = (xf * gain_ref[...]).astype(BF16)
+        ss = jnp.sum(xf * xf, axis=1, keepdims=True)
+        cbuf[k, m, :, :, :, QCOLS + 2 * KVCOLS : CW] = (
+            jnp.broadcast_to(ss, (256, 128)).astype(BF16).reshape(4, 4, HALF_ROWS, 128)
+        )
 
         def tile(n, _):
             cols = pl.ds(pl.multiple_of(n * 512, 512), 512)
             part = dot(ubuf[...], wall[:, cols])
-            cbuf[k, :, :, :, :, cols] = part.astype(BF16).reshape(4, 4, 2, HALF_ROWS, 512)
+            cbuf[k, m, :, :, :, cols] = part.astype(BF16).reshape(4, 4, HALF_ROWS, 512)
             return _
 
         lax.fori_loop(0, (QCOLS + 2 * KVCOLS) // 512, tile, 0)
@@ -207,6 +209,7 @@
             self.a1 = tracked(src(left, 0), fin(1, 0), dev(left))
             self.b0 = tracked(self.add0, fin(0, 0), dev(right))
             self.b1 = tracked(self.add1, fin(1, 1), dev(left))
+            self.copies = [self.f0, self.f1, self.a0, self.a1, self.b0, self.b1]
 
         def begin(self):
             for c in (self.f0, self.f1, self.a0, self.a1):
@@ -235,6 +238,7 @@
             self.l0 = tracked(block(i, 0), block(i, 0), dev(left))
             self.f0 = tracked(block(left, 0), block(left, 0), dev(right))
             self.f1 = tracked(block(right, 1), block(right, 1), dev(left))
+            self.copies = [self.r0, self.l1, self.r1, self.l0, self.f0, self.f1]
 
         def begin(self):
             for c in (self.r0, self.l1, self.r1, self.l0):
@@ -278,73 +282,85 @@
             for c in self.copies:
                 c.wait_recv()
 
-    def pool_rings(k):
+    def pool_rings(k, m):
+        def cols(n):
+            return slice(STARTS[n], STARTS[n] + WIDTHS[n])
+
+        def own(n):
+            return slice(0, WIDTHS[n])
+
         first = [
             RingSum(
                 z,
                 at_z,
-                lambda j, hf: cbuf.at[k, j, 2 * hf : 2 * hf + 2, 0],
-                lambda d: fwd1.at[k, 0, d],
-                lambda d, hf: fin1.at[k, 0, d, 2 * hf : 2 * hf + 2],
+                lambda j, hf: cbuf.at[k, m, j, 2 * hf : 2 * hf + 2, :, cols(0)],
+                lambda d: fwd1.at[k, m, 0, d, :, :, own(0)],
+                lambda d, hf: fin1.at[k, m, 0, d, 2 * hf : 2 * hf + 2, :, own(0)],
             ),
             RingSum(
                 y,
                 at_y,
-                lambda j, hf: cbuf.at[k, 2 * hf : 2 * hf + 2, j, 1],
-                lambda d: fwd1.at[k, 1, d],
-                lambda d, hf: fin1.at[k, 1, d, 2 * hf : 2 * hf + 2],
+                lambda j, hf: cbuf.at[k, m, 2 * hf : 2 * hf + 2, j, :, cols(1)],
+                lambda d: fwd1.at[k, m, 1, d, :, :, own(1)],
+                lambda d, hf: fin1.at[k, m, 1, d, 2 * hf : 2 * hf + 2, :, own(1)],
             ),
         ]
         second = [
             DirectSum(
-                (y, z)[h],
-                (at_y, at_z)[h],
-                lambda j, h=h: c2.at[k, h, j],
-                lambda n, h=h: fin2.at[k, h, n],
+                (y, z)[n],
+                (at_y, at_z)[n],
+                lambda j, n=n: c2.at[k, m, n, j, :, own(n)],
+                lambda c, n=n: fin2.at[k, m, n, c, :, own(n)],
             )
-            for h in range(2)
+            for n in range(2)
         ]
         return first, second
 
-    def sum_begin(k):
-        for r in rings[k][0]:
+    def sum_begin(k, m):
+        for r in rings[k][m][0]:
             r.begin()
 
-    def sum_middle(k):
-        for r in rings[k][0]:
+    def sum_middle(k, m):
+        for r in rings[k][m][0]:
             r.middle()
 
-    def sum_second(k):
-        first, second = rings[k]
-        for h in range(2):
-            first[h].end()
+    def sum_second(k, m):
+        first, second = rings[k][m]
+        for n in range(2):
+            first[n].end()
+            cols = slice(STARTS[n], STARTS[n] + WIDTHS[n])
+            own = slice(0, WIDTHS[n])
             for b in range(RING):
-                mine = cbuf[k, z, b, 0] if h == 0 else cbuf[k, b, y, 1]
-                c2[k, h, b] = (
+                mine = cbuf[k, m, z, b, :, cols] if n == 0 else cbuf[k, m, b, y, :, cols]
+                c2[k, m, n, b, :, own] = (
                     mine.astype(F32)
-                    + fin1[k, h, 0, b].astype(F32)
-                    + fin1[k, h, 1, b].astype(F32)
+                    + fin1[k, m, n, 0, b, :, own].astype(F32)
+                    + fin1[k, m, n, 1, b, :, own].astype(F32)
                 ).astype(BF16)
-            second[h].begin()
-
-    def sum_end(k):
-        for h in range(2):
-            rings[k][1][h].end()
-            total = c2[k, h, y if h == 0 else z].astype(F32)
-            for n in range(3):
-                total = total + fin2[k, h, n].astype(F32)
-            rstd = lax.rsqrt(total[:, QCOLS + 2 * KVCOLS :] * (1.0 / MODEL) + NORM_EPS)
-
-            def part(n):
-                return (total[:, n * HEAD : (n + 1) * HEAD] * rstd).astype(BF16).astype(F32)
-
-            keys = [part(HEADS + g) for g in range(2)]
-            values = [part(HEADS + 2 + g) for g in range(2)]
-            for n in range(HEADS):
-                at = pl.ds(h * HALF_ROWS * HEADS + n, HALF_ROWS, stride=HEADS)
-                qs[at, :] = part(n)
-                kns[at, :] = keys[n // 8]
-                vns[at, :] = values[n // 8]
+            second[n].begin()
+
+    def sum_end(k, m):
+        totals = []
+        for n in range(2):
+            rings[k][m][1][n].end()
+            own = slice(0, WIDTHS[n])
+            total = c2[k, m, n, y if n == 0 else z, :, own].astype(F32)
+            for c in range(3):
+                total = total + fin2[k, m, n, c, :, own].astype(F32)
+            totals.append(total)
+        total = jnp.concatenate(totals, axis=1)
+        rstd = lax.rsqrt(total[:, QCOLS + 2 * KVCOLS :] * (1.0 / MODEL) + NORM_EPS)
+
+        def part(n):
+            return (total[:, n * HEAD : (n + 1) * HEAD] * rstd).astype(BF16).astype(F32)
+
+        keys = [part(HEADS + g) for g in range(2)]
+        values = [part(HEADS + 2 + g) for g in range(2)]
+        for n in range(HEADS):
+            at = pl.ds(m * HALF_ROWS * HEADS + n, HALF_ROWS, stride=HEADS)
+            qs[at, :] = part(n)
+            kns[at, :] = keys[n // 8]
+            vns[at, :] = values[n // 8]
 
     inv_scale = 1.0 / math.sqrt(HEAD)
     group = 128 // HEADS
@@ -354,89 +370,94 @@
     position = lax.broadcasted_iota(jnp.int32, (2 * CTX, 128), 0)
     even = (position & 1) == 0
 
-    def attention(k):
-        for i in range(OWN_ROWS // group):
-            at = slice(i * 128, (i + 1) * 128)
-            q = qs[at, :]
-            own = jnp.exp(jnp.sum(q * kns[at, :], axis=1, keepdims=True) * inv_scale)
-            qt = q.T
-            wide = jnp.concatenate(
-                [jnp.where(low_heads, qt, 0.0), jnp.where(low_heads, 0.0, qt)], axis=0
+    def attention(k, i):
+        at = slice(i * 128, (i + 1) * 128)
+        q = qs[at, :]
+        own = jnp.exp(jnp.sum(q * kns[at, :], axis=1, keepdims=True) * inv_scale)
+        qt = q.T
+        wide = jnp.concatenate(
+            [jnp.where(low_heads, qt, 0.0), jnp.where(low_heads, 0.0, qt)], axis=0
+        )
+        length = jnp.zeros((1, 128), jnp.int32)
+        scores = jnp.zeros((2 * CTX, 128), F32)
+        for r in range(group):
+            mine = lane_row == r
+            scores = scores + dot(
+                kbuf[k, i * group + r], jnp.where(mine, wide, 0.0).astype(BF16)
             )
-            length = jnp.zeros((1, 128), jnp.int32)
-            scores = jnp.zeros((2 * CTX, 128), F32)
-            for r in range(group):
-                mine = lane_row == r
-                scores = scores + dot(
-                    kbuf[k, i * group + r], jnp.where(mine, wide, 0.0).astype(BF16)
-                )
-                length = jnp.where(
-                    mine, len_ref[s + 1 - k, p * OWN_ROWS + i * group + r], length
-                )
-            live = even & (position < 2 * length)
-            weights = jnp.where(live, jnp.exp(jnp.where(live, scores, 0.0) * inv_scale), 0.0)
-            weights = pltpu.roll(weights, 1, 0).T
-            den = jnp.sum(weights, axis=1, keepdims=True) + own
-            weights = weights.astype(BF16)
-            nums = []
-            for r in range(group):
-                pv = dot(weights[r * HEADS : (r + 1) * HEADS], kbuf[k, i * group + r])
-                nums += [pv[:8, :HEAD], pv[8:, HEAD:]]
-            num = jnp.concatenate(nums, axis=0) + own.astype(BF16).astype(F32) * vns[at, :]
-            att[at, :] = num / den
-        for h in range(2):
-            for n in range(HEADS):
-                at = pl.ds(h * HALF_ROWS * HEADS + n, HALF_ROWS, stride=HEADS)
-                agbuf[k, z, y, h, :, n * HEAD : (n + 1) * HEAD] = att[at, :].astype(BF16)
-
-    def gather_rings(k):
+            length = jnp.where(
+                mine, len_ref[s + 1 - k, p * OWN_ROWS + i * group + r], length
+            )
+        live = even & (position < 2 * length)
+        weights = jnp.where(live, jnp.exp(jnp.where(live, scores, 0.0) * inv_scale), 0.0)
+        weights = pltpu.roll(weights, 1, 0).T
+        den = jnp.sum(weights, axis=1, keepdims=True) + own
+        weights = weights.astype(BF16)
+        nums = []
+        for r in range(group):
+            pv = dot(weights[r * HEADS : (r + 1) * HEADS], kbuf[k, i * group + r])
+            nums += [pv[:8, :HEAD], pv[8:, HEAD:]]
+        num = jnp.concatenate(nums, axis=0) + own.astype(BF16).astype(F32) * vns[at, :]
+        att[at, :] = num / den
+
+    def attended(k, m):
+        for n in range(HEADS):
+            at = pl.ds(m * HALF_ROWS * HEADS + n, HALF_ROWS, stride=HEADS)
+            agbuf[k, m, z, y, :, n * HEAD : (n + 1) * HEAD] = att[at, :].astype(BF16)
+
+    def gather_rings(k, m):
+        low, high = slice(0, QCOLS // 2), slice(QCOLS // 2, QCOLS)
         first = [
-            DirectGather(y, at_y, lambda j: agbuf.at[k, z, j, 0]),
-            DirectGather(z, at_z, lambda j: agbuf.at[k, j, y, 1]),
+            DirectGather(y, at_y, lambda j: agbuf.at[k, m, z, j, :, low]),
+            DirectGather(z, at_z, lambda j: agbuf.at[k, m, j, y, :, high]),
         ]
         second = [
-            RingGather(z, at_z, lambda j, hf: agbuf.at[k, j, 2 * hf : 2 * hf + 2, 0]),
-            RingGather(y, at_y, lambda j, hf: agbuf.at[k, 2 * hf : 2 * hf + 2, j, 1]),
+            RingGather(
+                z, at_z, lambda j, hf: agbuf.at[k, m, j, 2 * hf : 2 * hf + 2, :, low]
+            ),
+            RingGather(
+                y, at_y, lambda j, hf: agbuf.at[k, m, 2 * hf : 2 * hf + 2, j, :, high]
+            ),
         ]
         return first, second
 
-    def gather_begin(k):
-        for r in gathers[k][0]:
+    def gather_begin(k, m):
+        for r in gathers[k][m][0]:
             r.begin()
 
-    def gather_second(k):
-        first, second = gathers[k]
-        for h in range(2):
-            first[h].end()
-            second[h].begin()
-
-    def gather_end(k):
-        second = gathers[k][1]
-        for r in second:
+    def gather_second(k, m):
+        first, second = gathers[k][m]
+        for n in range(2):
+            first[n].end()
+            second[n].begin()
+
+    def gather_middle(k, m):
+        for r in gathers[k][m][1]:
             r.middle()
-        for r in second:
+
+    def gather_end(k, m):
+        for r in gathers[k][m][1]:
             r.end()
 
-    def output_products(k):
-        for pair in ((2, 1), (3, 0)):
-            chunks = [ring(t, d) for d in pair]
-            rows = jnp.concatenate([agbuf[k, j].reshape(128, QCOLS) for j in chunks], axis=0)
-            both = dot(rows, wo[...])
-            for n, j in enumerate(chunks):
-                ob[k, j] = both[n * 128 : (n + 1) * 128, :FEAT].astype(BF16)
-                down = both[n * 128 : (n + 1) * 128, FEAT:].T
-                ids = rslot[pl.ds(k, 1), pl.ds(pl.multiple_of(j * 128, 128), 128)]
-                acc = jnp.zeros((RANK, 128), F32)
-                for m in range(16):
-                    slot = ((s if m < 8 else o) * 16 + p) * 8 + m % 8
-                    acc = acc + jnp.where(
-                        ids == slot, down[m * RANK : (m + 1) * RANK, :], 0.0
-                    )
-                lrown[k, j] = acc
-            for d in pair:
-                if d > 0:
-                    lows[k][d - 1].start()
-                    tops[k][d - 1].start()
+    def down_product(k, m):
+        rows = agbuf[k, m].reshape(256, QCOLS)
+        down = dot(rows, wo[:, FEAT:]).T
+        ids = half_slot[k, m, 0:1, :]
+        acc = jnp.zeros((RANK, 256), F32)
+        for n in range(16):
+            slot = ((s if n < 8 else o) * 16 + p) * 8 + n % 8
+            acc = acc + jnp.where(ids == slot, down[n * RANK : (n + 1) * RANK, :], 0.0)
+        for j in range(RING):
+            lrown[k, j, :, m * 64 : (m + 1) * 64] = acc[:, j * 64 : (j + 1) * 64]
+        if m == 1:
+            for c in lows[k]:
+                c.start()
+
+    def out_product(k, m):
+        rows = agbuf[k, m].reshape(256, QCOLS)
+        ob[k, m] = dot(rows, wo[:, :FEAT]).astype(BF16).reshape(4, 4, HALF_ROWS, FEAT)
+        for d in (2, 1, 3):
+            tops[k][m][d - 1].start()
 
     def output_low(k):
         total = lrown[k, t]
@@ -476,20 +497,25 @@
             low_rank = low_rank + lrp[k, n].astype(F32)
         for c in panels[k]:
             c.wait_recv()
-        ids = rslot[pl.ds(k, 1), pl.ds(pl.multiple_of(t * 128, 128), 128)]
+        ids = chunk_slot[k, t, 0:1, :]
         block = lax.shift_right_logical(ids, 3)
         wide = jnp.concatenate(
             [jnp.where(block == b, low_rank, 0.0) for b in range(32)], axis=0
         )
         delta = dot(wide.T.astype(BF16), upbuf[k].reshape(512, FEAT))
-        row = pl.ds(pl.multiple_of(t * 128, 128), 128)
-        total = (
-            xin[k, row, :].astype(F32) + ob[k, t].astype(F32) + ADAPTER_SCALE * delta
-        )
-        for d in range(1, RING):
-            tops[k][d - 1].wait_recv()
-            total = total + finx[k, d - 1].astype(F32)
-        outs[k][0] = total.astype(BF16)
+        for m in range(2):
+            for c in tops[k][m]:
+                c.wait_recv()
+            for b in range(4):
+                at = b * OWN_ROWS + m * HALF_ROWS
+                row = pl.ds(pl.multiple_of(t * 128, 128) + at, HALF_ROWS)
+                total = xin[k, row, :].astype(F32) + ob[k, m, t, b].astype(F32)
+                for d in range(3):
+                    total = total + finx[k, m, d, b].astype(F32)
+                from_row = m * 64 + b * HALF_ROWS
+                outs[k][0, at : at + HALF_ROWS, :] = (
+                    total + ADAPTER_SCALE * delta[from_row : from_row + HALF_ROWS]
+                ).astype(BF16)
 
     def slots_and_offsets():
         ids = [aor_ref[pl.ds(s + 1 - k, 1), :] for k in range(2)]
@@ -517,12 +543,37 @@
             ((jnp.zeros((1, ROWS), jnp.int32),) * 2, (jnp.int32(0),) * 12),
         )
         for k in range(2):
-            rslot[pl.ds(k, 1), :] = rows[k]
+
+            def piece(j, b, m):
+                at = (j * RING + b) * OWN_ROWS + m * HALF_ROWS
+                return rows[k][:, at : at + HALF_ROWS]
+
+            for m in range(2):
+                half_slot[k, m, 0:1, :] = jnp.concatenate(
+                    [piece(j, b, m) for j in range(RING) for b in range(RING)], axis=1
+                )
+            for j in range(RING):
+                chunk_slot[k, j, 0:1, :] = jnp.concatenate(
+                    [piece(j, b, m) for m in range(2) for b in range(RING)], axis=1
+                )
         return offs
 
-    def give_panels(offs):
-        got = [[], []]
-        mine = s * RING + t
+    panels = [[], []]
+    holder = s * RING + t
+    for w in range(2):
+        for k in range(2):
+            for d in range(1 if w == 0 else 0, RING):
+                panels[k].append(
+                    tracked(
+                        sel.at[w, k],
+                        upbuf.at[k, holder],
+                        {"section": s if w == 0 else o, "tensor": ring(t, d)},
+                    )
+                )
+
+    def slots_and_panels():
+        offs = slots_and_offsets()
+        load_up.wait()
         for w in range(2):
             layer = s if w == 0 else o
             for k in range(2):
@@ -530,16 +581,10 @@
                     off = jnp.where(layer == 0, offs[4 * (1 - k) + j], offs[4 * (2 - k) + j])
                     sel[w, k, j * RANK : (j + 1) * RANK, :] = upv[8 * j + off, layer]
                 if w == 0:
-                    upbuf[k, mine] = sel[w, k]
-                for d in range(1 if w == 0 else 0, RING):
-                    got[k].append(
-                        send(
-                            sel.at[w, k],
-                            upbuf.at[k, mine],
-                            {"section": layer, "tensor": ring(t, d)},
-                        )
-                    )
-        return got
+                    upbuf[k, holder] = sel[w, k]
+        for k in range(2):
+            for c in panels[k]:
+                c.start()
 
     def spread_down():
         for n in range(2):
@@ -549,8 +594,8 @@
                     panel.astype(F32).T.astype(BF16)
                 )
 
-    rings = [pool_rings(k) for k in range(2)]
-    gathers = [gather_rings(k) for k in range(2)]
+    rings = [[pool_rings(k, m) for m in range(2)] for k in range(2)]
+    gathers = [[gather_rings(k, m) for m in range(2)] for k in range(2)]
     lows = [
         [
             tracked(lrown.at[k, ring(t, d)], lrx.at[k, t], at_x(ring(t, d)))
@@ -560,11 +605,28 @@
     ]
     tops = [
         [
-            tracked(ob.at[k, ring(t, d)], finx.at[k, d - 1], at_x(ring(t, d)))
-            for d in range(1, RING)
+            [
+                tracked(ob.at[k, m, ring(t, d)], finx.at[k, m, d - 1], at_x(ring(t, d)))
+                for d in range(1, RING)
+            ]
+            for m in range(2)
         ]
         for k in range(2)
     ]
+
+    def drain(copies):
+        for c in copies:
+            c.wait_send()
+            started[:] = [other for other in started if other is not c]
+
+    def ring_copies(which):
+        return [
+            c
+            for m in range(2)
+            for stage in which[m]
+            for r in stage
+            for c in r.copies
+        ]
 
     load_x0.wait()
     load_wq.wait()
@@ -578,41 +640,67 @@
     load_wo.start()
     load_dn.start()
     load_c[1].start()
-    project(0)
+    project(0, 0)
     pl.semaphore_wait(barrier, 22)
     other_down = send(down_hbm.at[:, o], dn.at[1], {"section": o})
 
     @pl.when(s == 1)
     def _():
+        project(0, 1)
+        slots_and_panels()
         pl.semaphore_wait(turn, 1)
 
-    sum_begin(0)
-    offs = slots_and_offsets()
-    sum_middle(0)
+    sum_begin(0, 0)
 
     @pl.when(s == 0)
     def _():
-        load_fresh.wait()
-        project(1)
-
-    sum_second(0)
-    load_up.wait()
-    panels = give_panels(offs)
-    sum_end(0)
+        project(0, 1)
+
+    sum_middle(0, 0)
+    sum_begin(0, 1)
 
     @pl.when(s == 0)
     def _():
-        pl.semaphore_signal(turn, inc=1, device_id={"section": o}, device_id_type=MESH)
-
-    load_c[0].wait()
-    attention(0)
-    gather_begin(0)
+        slots_and_panels()
+
+    sum_second(0, 0)
+    sum_middle(0, 1)
     load_dn.wait()
     other_down.wait_recv()
     load_wo.wait()
     spread_down()
-    gather_second(0)
-    gather_end(0)
+    sum_end(0, 0)
+    sum_second(0, 1)
+
+    @pl.when(s == 0)
+    def _():
+        pl.semaphore_signal(turn, inc=1, device_id={"section": o}, device_id_type=MESH)
+
+    load_c[0].wait()
+    attention(0, 0)
+    attention(0, 1)
+    attended(0, 0)
+    gather_begin(0, 0)
+    sum_end(0, 1)
+    attention(0, 2)
+    gather_second(0, 0)
+    attention(0, 3)
+    attended(0, 1)
+    gather_begin(0, 1)
+    gather_middle(0, 0)
+    gather_second(0, 1)
+
+    @pl.when(s == 0)
+    def _():
+        load_fresh.wait()
+        project(1, 0)
+
+    gather_end(0, 0)
+    down_product(0, 0)
+    gather_middle(0, 1)
+    out_product(0, 0)
+    gather_end(0, 1)
+    down_product(0, 1)
 
     row = pl.ds(pl.multiple_of(t * 128, 128), 128)
     relay = [
@@ -624,20 +712,17 @@
     def _():
         for c in relay:
             c.wait_recv()
-        project(1)
-
-    sum_begin(1)
-    output_products(0)
+        project(1, 0)
+
+    sum_begin(1, 0)
+    out_product(0, 1)
+    output_low(0)
 
     @pl.when(s == 1)
     def _():
-        sum_middle(1)
-
-    output_low(0)
-
-    @pl.when(s == 1)
-    def _():
-        sum_second(1)
+        project(1, 1)
+        sum_middle(1, 0)
+        sum_begin(1, 1)
 
     output_delta(0)
 
@@ -645,22 +730,44 @@
     def _():
         for d in (2, 1, 3, 0):
             relay[d].start()
-        sum_middle(1)
-        sum_second(1)
+        project(1, 1)
+        sum_middle(1, 0)
+        sum_begin(1, 1)
         for c in relay:
             c.wait_send()
 
-    sum_end(1)
+    drain(ring_copies(rings[0]))
+    sum_second(1, 0)
+    sum_middle(1, 1)
+    drain(ring_copies(gathers[0]))
+    drain([other_down] + lows[0] + tops[0][0] + tops[0][1] + panels[0] + panels[1])
+    sum_end(1, 0)
+    sum_second(1, 1)
     load_c[1].wait()
-    attention(1)
-    gather_begin(1)
-    gather_second(1)
-    gather_end(1)
-    output_products(1)
+    attention(1, 0)
+    attention(1, 1)
+    attended(1, 0)
+    gather_begin(1, 0)
+    sum_end(1, 1)
+    attention(1, 2)
+    gather_second(1, 0)
+    attention(1, 3)
+    attended(1, 1)
+    gather_begin(1, 1)
+    gather_middle(1, 0)
+    gather_second(1, 1)
+    drain(ring_copies(rings[1]))
+    gather_end(1, 0)
+    down_product(1, 0)
+    gather_middle(1, 1)
+    out_product(1, 0)
+    gather_end(1, 1)
+    down_product(1, 1)
+    out_product(1, 1)
     output_low(1)
+    drain(ring_copies(gathers[1]))
     output_delta(1)
-    for c in started:
-        c.wait_send()
+    drain(list(started))
 
 
 def hand_over(first_in, second_in, first_out, second_out):
@@ -703,17 +810,18 @@
             v((2, 2, 4 * RANK, FEAT), BF16),
             v((2, 8, 4 * RANK, FEAT), BF16),
             v((2, OWN_ROWS, 2 * CTX, KVCOLS), BF16),
-            v((2, RING, RING, 2, HALF_ROWS, CW), BF16),
-            v((2, 2, 2, 2, HALF_ROWS, CW), BF16),
-            v((2, 2, 2, RING, HALF_ROWS, CW), BF16),
-            v((2, 2, RING, HALF_ROWS, CW), BF16),
-            v((2, 2, 3, HALF_ROWS, CW), BF16),
-            v((2, RING, RING, 2, HALF_ROWS, QCOLS), BF16),
-            v((2, RING, 128, FEAT), BF16),
-            v((2, 3, 128, FEAT), BF16),
+            v((2, 2, RING, RING, HALF_ROWS, CW), BF16),
+            v((2, 2, 2, 2, 2, HALF_ROWS, WIDTHS[0]), BF16),
+            v((2, 2, 2, 2, RING, HALF_ROWS, WIDTHS[0]), BF16),
+            v((2, 2, 2, RING, HALF_ROWS, WIDTHS[0]), BF16),
+            v((2, 2, 2, 3, HALF_ROWS, WIDTHS[0]), BF16),
+            v((2, 2, RING, RING, HALF_ROWS, QCOLS), BF16),
+            v((2, 2, RING, RING, HALF_ROWS, FEAT), BF16),
+            v((2, 2, 3, RING, HALF_ROWS, FEAT), BF16),
             v((2, ROWS, FEAT), BF16),
-            v((ROWS, FEAT), BF16),
-            v((8, ROWS), jnp.int32),
+            v((ROWS // 2, FEAT), BF16),
+            v((2, 2, 8, 256), jnp.int32),
+            v((2, RING, 8, 128), jnp.int32),
             v((OWN_ROWS * HEADS, HEAD), F32),
             v((OWN_ROWS * HEADS, HEAD), F32),
             v((OWN_ROWS * HEADS, HEAD), F32),

time: 111 us -> 108 us (0.973)
  Pallas kernels: 110 us -> 107 us
    pallas_call x1, Pallas kernels: 108 us -> 106 us  [on_device(): pl.pallas_call(kernel, out_shape=(out, out), in_specs=[any_space, any_spa...]
where the time goes in v2:
time: 108 us
  Pallas kernels  107 us (99%)
    pallas_call x1, Pallas kernels, on_device(): pl.pallas_call(kernel, out_shape=(out, out), in_specs=[any_space, any_spa...  106 us

profile of v2, /device:TPU:1, one launch (start us, length us, event | category | flops | bytes accessed | tf_op | source)
XLA Modules:
  0.0 108.1 jit_solution(12828015331713543752)
XLA Ops:
  0.6 105.8 %shard_map.140 = (bf16[1,128,512]{2,1,0:T(8,128)(2,1)}, bf16[1,128,512]{2,1,0:T(8,128)(2,1)}) custom-call(bf16[1,512,512]{2,1,0:T(8,128)(2,1)} %hidden_hbm.1, bf16[512,512]{1,0:T(8,128)(2,1)} %fresh_hbm.1, f32[1,512]{1,0:T(1,128)} %gain_ref.1, bf16[1,512,2048]{2,1,0:T(8,128)(2,1)} %wq_hbm.1, bf16[1,512,2,256]{3,2,1,0:T(2,128)(2,1)} %wkv_hbm.1, ...), custom_call_target="tpu_custom_call" | custom-call | flops 8000000000 | bytes 16000000 | tf_op jit(solution)/shard_map/pallas_call | solution.py:785
  106.4 1.7 %shard_map.141 = (bf16[1,128,512]{2,1,0:T(8,128)(2,1)}, bf16[1,128,512]{2,1,0:T(8,128)(2,1)}) custom-call(bf16[1,128,512]{2,1,0:T(8,128)(2,1)} %get-tuple-element.4.first_in, bf16[1,128,512]{2,1,0:T(8,128)(2,1)} %get-tuple-element.5.second_in), custom_call_target="tpu_custom_call" | custom-call | tf_op jit(solution)/shard_map/pallas_call | solution.py:846

commit v3 on v2

--- a/solution.py
+++ b/solution.py
@@ -181,7 +181,7 @@
                 QCOLS + n * KVCOLS : QCOLS + (n + 1) * KVCOLS,
             ] = dot(pick, block).astype(BF16)
 
-    def project(k, m):
+    def project(k, m, begin=False, ready=None):
         base = [q * OWN_ROWS + m * HALF_ROWS for q in range(16)]
         xf = jnp.concatenate([xin[k, b : b + HALF_ROWS, :] for b in base], axis=0).astype(F32)
         ubuf[...] = (xf * gain_ref[...]).astype(BF16)
@@ -196,7 +196,14 @@
             cbuf[k, m, :, :, :, cols] = part.astype(BF16).reshape(4, 4, HALF_ROWS, 512)
             return _
 
-        lax.fori_loop(0, (QCOLS + 2 * KVCOLS) // 512, tile, 0)
+        lax.fori_loop(0, 3, tile, 0)
+        if ready is not None:
+            ready()
+        if begin:
+            rings[k][m][0][0].begin()
+        lax.fori_loop(3, 5, tile, 0)
+        if begin:
+            rings[k][m][0][1].begin()
 
     class RingSum:
         def __init__(self, i, dev, src, fwd, fin):
@@ -571,8 +578,7 @@
                     )
                 )
 
-    def slots_and_panels():
-        offs = slots_and_offsets()
+    def give_panels(offs):
         load_up.wait()
         for w in range(2):
             layer = s if w == 0 else o
@@ -640,35 +646,39 @@
     load_wo.start()
     load_dn.start()
     load_c[1].start()
-    project(0, 0)
-    pl.semaphore_wait(barrier, 22)
-    other_down = send(down_hbm.at[:, o], dn.at[1], {"section": o})
+    other_down = tracked(down_hbm.at[:, o], dn.at[1], {"section": o})
+
+    def everyone_is_here():
+        pl.semaphore_wait(barrier, 22)
+
+    @pl.when(s == 0)
+    def _():
+        project(0, 0, begin=True, ready=everyone_is_here)
+        other_down.start()
+        project(0, 1)
+        sum_middle(0, 0)
+        sum_begin(0, 1)
+        offs = slots_and_offsets()
+        sum_middle(0, 1)
+        sum_second(0, 0)
+        give_panels(offs)
+        load_fresh.wait()
+        project(1, 0)
 
     @pl.when(s == 1)
     def _():
+        project(0, 0)
+        everyone_is_here()
+        other_down.start()
         project(0, 1)
-        slots_and_panels()
+        give_panels(slots_and_offsets())
         pl.semaphore_wait(turn, 1)
-
-    sum_begin(0, 0)
-
-    @pl.when(s == 0)
-    def _():
-        project(0, 1)
-
-    sum_middle(0, 0)
-    sum_begin(0, 1)
-
-    @pl.when(s == 0)
-    def _():
-        slots_and_panels()
-
-    sum_second(0, 0)
-    sum_middle(0, 1)
-    load_dn.wait()
-    other_down.wait_recv()
-    load_wo.wait()
-    spread_down()
+        sum_begin(0, 0)
+        sum_middle(0, 0)
+        sum_begin(0, 1)
+        sum_middle(0, 1)
+        sum_second(0, 0)
+
     sum_end(0, 0)
     sum_second(0, 1)
 
@@ -689,15 +699,13 @@
     gather_begin(0, 1)
     gather_middle(0, 0)
     gather_second(0, 1)
-
-    @pl.when(s == 0)
-    def _():
-        load_fresh.wait()
-        project(1, 0)
-
+    load_dn.wait()
+    other_down.wait_recv()
+    load_wo.wait()
+    spread_down()
     gather_end(0, 0)
+    gather_middle(0, 1)
     down_product(0, 0)
-    gather_middle(0, 1)
     out_product(0, 0)
     gather_end(0, 1)
     down_product(0, 1)
@@ -708,26 +716,12 @@
         for d in range(RING)
     ]
 
-    @pl.when(s == 1)
-    def _():
-        for c in relay:
-            c.wait_recv()
-        project(1, 0)
-
-    sum_begin(1, 0)
-    out_product(0, 1)
-    output_low(0)
-
-    @pl.when(s == 1)
-    def _():
-        project(1, 1)
-        sum_middle(1, 0)
-        sum_begin(1, 1)
-
-    output_delta(0)
-
     @pl.when(s == 0)
     def _():
+        out_product(0, 1)
+        sum_begin(1, 0)
+        output_low(0)
+        output_delta(0)
         for d in (2, 1, 3, 0):
             relay[d].start()
         project(1, 1)
@@ -735,12 +729,22 @@
         sum_begin(1, 1)
         for c in relay:
             c.wait_send()
-
-    drain(ring_copies(rings[0]))
-    sum_second(1, 0)
-    sum_middle(1, 1)
-    drain(ring_copies(gathers[0]))
-    drain([other_down] + lows[0] + tops[0][0] + tops[0][1] + panels[0] + panels[1])
+        sum_middle(1, 1)
+        sum_second(1, 0)
+
+    @pl.when(s == 1)
+    def _():
+        for c in relay:
+            c.wait_recv()
+        project(1, 0, begin=True)
+        project(1, 1)
+        sum_middle(1, 0)
+        sum_begin(1, 1)
+        out_product(0, 1)
+        sum_middle(1, 1)
+        sum_second(1, 0)
+        output_low(0)
+
     sum_end(1, 0)
     sum_second(1, 1)
     load_c[1].wait()
@@ -755,16 +759,24 @@
     attended(1, 1)
     gather_begin(1, 1)
     gather_middle(1, 0)
+    drain(ring_copies(rings[0]))
     gather_second(1, 1)
-    drain(ring_copies(rings[1]))
+
+    @pl.when(s == 1)
+    def _():
+        output_delta(0)
+
     gather_end(1, 0)
+    gather_middle(1, 1)
+    drain(ring_copies(gathers[0]))
     down_product(1, 0)
-    gather_middle(1, 1)
     out_product(1, 0)
+    drain([other_down] + lows[0] + tops[0][0] + tops[0][1] + panels[0] + panels[1])
     gather_end(1, 1)
     down_product(1, 1)
     out_product(1, 1)
     output_low(1)
+    drain(ring_copies(rings[1]))
     drain(ring_copies(gathers[1]))
     output_delta(1)
     drain(list(started))

time: 108 us -> 110 us (1.019)
  Pallas kernels: 107 us -> 109 us
    pallas_call x1, Pallas kernels: 106 us -> 107 us  [on_device(): pl.pallas_call(kernel, out_shape=(out, out), in_specs=[any_space, any_spa...]
where the time goes in v3:
time: 110 us
  Pallas kernels  109 us (99%)
    pallas_call x1, Pallas kernels, on_device(): pl.pallas_call(kernel, out_shape=(out, out), in_specs=[any_space, any_spa...  107 us

profile of v3, /device:TPU:1, one launch (start us, length us, event | category | flops | bytes accessed | tf_op | source)
XLA Modules:
  0.0 109.8 jit_solution(4551351828999368773)
XLA Ops:
  0.6 107.4 %shard_map.140 = (bf16[1,128,512]{2,1,0:T(8,128)(2,1)}, bf16[1,128,512]{2,1,0:T(8,128)(2,1)}) custom-call(bf16[1,512,512]{2,1,0:T(8,128)(2,1)} %hidden_hbm.1, bf16[512,512]{1,0:T(8,128)(2,1)} %fresh_hbm.1, f32[1,512]{1,0:T(1,128)} %gain_ref.1, bf16[1,512,2048]{2,1,0:T(8,128)(2,1)} %wq_hbm.1, bf16[1,512,2,256]{3,2,1,0:T(2,128)(2,1)} %wkv_hbm.1, ...), custom_call_target="tpu_custom_call" | custom-call | flops 8000000000 | bytes 16000000 | tf_op jit(solution)/shard_map/pallas_call | solution.py:797
  108.1 1.7 %shard_map.141 = (bf16[1,128,512]{2,1,0:T(8,128)(2,1)}, bf16[1,128,512]{2,1,0:T(8,128)(2,1)}) custom-call(bf16[1,128,512]{2,1,0:T(8,128)(2,1)} %get-tuple-element.4.first_in, bf16[1,128,512]{2,1,0:T(8,128)(2,1)} %get-tuple-element.5.second_in), custom_call_target="tpu_custom_call" | custom-call | tf_op jit(solution)/shard_map/pallas_call | solution.py:858

commit v4 on v3

--- a/solution.py
+++ b/solution.py
@@ -134,7 +134,10 @@
 
     kvflat = wkv_hbm.reshape(2 * FEAT, KVCOLS)
     cflat = cache_hbm.reshape(2, OWN_ROWS, 2 * CTX, KVCOLS)
-    load_x0 = pltpu.make_async_copy(hidden_hbm.at[0], xin.at[0], lsem.at[0])
+    load_x0 = [
+        pltpu.make_async_copy(hidden_hbm.at[:, :, m], xin.at[0, m], lsem.at[(0, 9)[m]])
+        for m in range(2)
+    ]
     load_kv = pltpu.make_async_copy(kvflat, kvraw, lsem.at[1])
     load_wq = pltpu.make_async_copy(wq_hbm.at[0], wall.at[:, 0:QCOLS], lsem.at[2])
     load_up = pltpu.make_async_copy(up_hbm, upv, lsem.at[3])
@@ -143,10 +146,14 @@
         pltpu.make_async_copy(cflat.at[k], kbuf.at[k], lsem.at[5 + k]) for k in range(2)
     ]
     load_wo = pltpu.make_async_copy(wo_hbm.at[0], wo.at[:, 0:FEAT], lsem.at[7])
-    load_x0.start()
+    for c in load_x0:
+        c.start()
     load_kv.start()
     load_wq.start()
-    load_fresh = pltpu.make_async_copy(fresh_hbm, xin.at[1], lsem.at[8])
+    load_fresh = [
+        pltpu.make_async_copy(fresh_hbm.at[:, :, m], xin.at[1, m], lsem.at[(8, 10)[m]])
+        for m in range(2)
+    ]
 
     barrier = pltpu.get_barrier_semaphore()
 
@@ -182,8 +189,7 @@
             ] = dot(pick, block).astype(BF16)
 
     def project(k, m, begin=False, ready=None):
-        base = [q * OWN_ROWS + m * HALF_ROWS for q in range(16)]
-        xf = jnp.concatenate([xin[k, b : b + HALF_ROWS, :] for b in base], axis=0).astype(F32)
+        xf = xin[k, m].reshape(256, FEAT).astype(F32)
         ubuf[...] = (xf * gain_ref[...]).astype(BF16)
         ss = jnp.sum(xf * xf, axis=1, keepdims=True)
         cbuf[k, m, :, :, :, QCOLS + 2 * KVCOLS : CW] = (
@@ -454,11 +460,11 @@
         for n in range(16):
             slot = ((s if n < 8 else o) * 16 + p) * 8 + n % 8
             acc = acc + jnp.where(ids == slot, down[n * RANK : (n + 1) * RANK, :], 0.0)
+        pad = jnp.zeros((RANK, 64), F32)
         for j in range(RING):
-            lrown[k, j, :, m * 64 : (m + 1) * 64] = acc[:, j * 64 : (j + 1) * 64]
-        if m == 1:
-            for c in lows[k]:
-                c.start()
+            lrown[k, m, j] = jnp.concatenate([acc[:, j * 64 : (j + 1) * 64], pad], axis=1)
+        for c in lows[k][m]:
+            c.start()
 
     def out_product(k, m):
         rows = agbuf[k, m].reshape(256, QCOLS)
@@ -466,63 +472,54 @@
         for d in (2, 1, 3):
             tops[k][m][d - 1].start()
 
-    def output_low(k):
-        total = lrown[k, t]
+    def low_copy(k, m, d):
+        return pltpu.make_async_remote_copy(
+            src_ref=lrp.at[k, m, p],
+            dst_ref=lrp.at[k, m, p],
+            send_sem=psend.at[k, m, d],
+            recv_sem=precv.at[k, m, d],
+            device_id={"pool": lax.rem(p + d, 16)},
+            device_id_type=MESH,
+        )
+
+    def output_low(k, m):
+        total = lrown[k, m, t]
         for d in range(1, RING):
-            lows[k][d - 1].wait_recv()
-            total = total + lrx[k, ring(t, -d)]
-        lrp[k, p] = total.astype(BF16)
+            lows[k][m][d - 1].wait_recv()
+            total = total + lrx[k, m, ring(t, -d)]
+        lrp[k, m, p] = total.astype(BF16)
 
         def give(d, _):
-            pltpu.make_async_remote_copy(
-                src_ref=lrp.at[k, p],
-                dst_ref=lrp.at[k, p],
-                send_sem=psend.at[k, d],
-                recv_sem=precv.at[k, d],
-                device_id={"pool": lax.rem(p + d, 16)},
-                device_id_type=MESH,
-            ).start()
+            low_copy(k, m, d).start()
             return _
 
         lax.fori_loop(1, 16, give, 0)
 
-    def output_delta(k):
-        def take(d, _):
-            pltpu.make_async_remote_copy(
-                src_ref=lrp.at[k, p],
-                dst_ref=lrp.at[k, p],
-                send_sem=psend.at[k, d],
-                recv_sem=precv.at[k, d],
-                device_id={"pool": lax.rem(p + d, 16)},
-                device_id_type=MESH,
-            ).wait()
+    def output_delta(k, m):
+        def receive(d, _):
+            low_copy(k, m, d).wait()
             return _
 
-        lax.fori_loop(1, 16, take, 0)
-        low_rank = lrp[k, 0].astype(F32)
+        lax.fori_loop(1, 16, receive, 0)
+        low_rank = lrp[k, m, 0].astype(F32)
         for n in range(1, 16):
-            low_rank = low_rank + lrp[k, n].astype(F32)
-        for c in panels[k]:
-            c.wait_recv()
-        ids = chunk_slot[k, t, 0:1, :]
-        block = lax.shift_right_logical(ids, 3)
+            low_rank = low_rank + lrp[k, m, n].astype(F32)
+        if m == 0:
+            for c in panels[k]:
+                c.wait_recv()
+        block = lax.shift_right_logical(chunk_slot[k, m, t, 0:1, :], 3)
         wide = jnp.concatenate(
             [jnp.where(block == b, low_rank, 0.0) for b in range(32)], axis=0
         )
-        delta = dot(wide.T.astype(BF16), upbuf[k].reshape(512, FEAT))
-        for m in range(2):
-            for c in tops[k][m]:
-                c.wait_recv()
-            for b in range(4):
-                at = b * OWN_ROWS + m * HALF_ROWS
-                row = pl.ds(pl.multiple_of(t * 128, 128) + at, HALF_ROWS)
-                total = xin[k, row, :].astype(F32) + ob[k, m, t, b].astype(F32)
-                for d in range(3):
-                    total = total + finx[k, m, d, b].astype(F32)
-                from_row = m * 64 + b * HALF_ROWS
-                outs[k][0, at : at + HALF_ROWS, :] = (
-                    total + ADAPTER_SCALE * delta[from_row : from_row + HALF_ROWS]
-                ).astype(BF16)
+        delta = dot(wide.T[:64].astype(BF16), upbuf[k].reshape(512, FEAT))
+        total = xin[k, m, t].astype(F32) + ob[k, m, t].astype(F32)
+        for c in tops[k][m]:
+            c.wait_recv()
+        for d in range(3):
+            total = total + finx[k, m, d].astype(F32)
+        outs[k][0, :, m] = (
+            total + ADAPTER_SCALE * delta.reshape(RING, HALF_ROWS, FEAT)
+        ).astype(BF16)
 
     def slots_and_offsets():
         ids = [aor_ref[pl.ds(s + 1 - k, 1), :] for k in range(2)]
@@ -559,10 +556,9 @@
                 half_slot[k, m, 0:1, :] = jnp.concatenate(
                     [piece(j, b, m) for j in range(RING) for b in range(RING)], axis=1
                 )
-            for j in range(RING):
-                chunk_slot[k, j, 0:1, :] = jnp.concatenate(
-                    [piece(j, b, m) for m in range(2) for b in range(RING)], axis=1
-                )
+                for j in range(RING):
+                    part = jnp.concatenate([piece(j, b, m) for b in range(RING)], axis=1)
+                    chunk_slot[k, m, j, 0:1, :] = jnp.concatenate([part, part], axis=1)
         return offs
 
     panels = [[], []]
@@ -604,8 +600,11 @@
     gathers = [[gather_rings(k, m) for m in range(2)] for k in range(2)]
     lows = [
         [
-            tracked(lrown.at[k, ring(t, d)], lrx.at[k, t], at_x(ring(t, d)))
-            for d in range(1, RING)
+            [
+                tracked(lrown.at[k, m, ring(t, d)], lrx.at[k, m, t], at_x(ring(t, d)))
+                for d in range(1, RING)
+            ]
+            for m in range(2)
         ]
         for k in range(2)
     ]
@@ -634,14 +633,16 @@
             for c in r.copies
         ]
 
-    load_x0.wait()
+    for c in load_x0:
+        c.wait()
     load_wq.wait()
     load_up.start()
     load_c[0].start()
 
     @pl.when(s == 0)
     def _():
-        load_fresh.start()
+        for c in load_fresh:
+            c.start()
 
     load_wo.start()
     load_dn.start()
@@ -662,7 +663,8 @@
         sum_middle(0, 1)
         sum_second(0, 0)
         give_panels(offs)
-        load_fresh.wait()
+        for c in load_fresh:
+            c.wait()
         project(1, 0)
 
     @pl.when(s == 1)
@@ -705,45 +707,68 @@
     spread_down()
     gather_end(0, 0)
     gather_middle(0, 1)
+
+    @pl.when(s == 0)
+    def _():
+        sum_begin(1, 0)
+        project(1, 1)
+
     down_product(0, 0)
     out_product(0, 0)
-    gather_end(0, 1)
-    down_product(0, 1)
-
-    row = pl.ds(pl.multiple_of(t * 128, 128), 128)
+
     relay = [
-        remote(first_ref.at[0], xin.at[1, row], {"section": 1, "tensor": ring(t, d)})
-        for d in range(RING)
+        [
+            remote(
+                first_ref.at[0, :, m], xin.at[1, m, t], {"section": 1, "tensor": ring(t, d)}
+            )
+            for d in range(RING)
+        ]
+        for m in range(2)
     ]
+
+    def relay_start(m):
+        for d in (2, 1, 3, 0):
+            relay[m][d].start()
+
+    def relay_wait(m):
+        for c in relay[m]:
+            c.wait_recv()
 
     @pl.when(s == 0)
     def _():
-        out_product(0, 1)
-        sum_begin(1, 0)
-        output_low(0)
-        output_delta(0)
-        for d in (2, 1, 3, 0):
-            relay[d].start()
-        project(1, 1)
-        sum_middle(1, 0)
-        sum_begin(1, 1)
-        for c in relay:
-            c.wait_send()
-        sum_middle(1, 1)
-        sum_second(1, 0)
-
-    @pl.when(s == 1)
-    def _():
-        for c in relay:
-            c.wait_recv()
-        project(1, 0, begin=True)
-        project(1, 1)
+        output_low(0, 0)
+        gather_end(0, 1)
+        down_product(0, 1)
+        output_delta(0, 0)
+        relay_start(0)
         sum_middle(1, 0)
         sum_begin(1, 1)
         out_product(0, 1)
+        output_low(0, 1)
         sum_middle(1, 1)
+        output_delta(0, 1)
+        relay_start(1)
         sum_second(1, 0)
-        output_low(0)
+        for m in range(2):
+            for c in relay[m]:
+                c.wait_send()
+
+    @pl.when(s == 1)
+    def _():
+        output_low(0, 0)
+        gather_end(0, 1)
+        relay_wait(0)
+        project(1, 0, begin=True)
+        down_product(0, 1)
+        sum_middle(1, 0)
+        relay_wait(1)
+        project(1, 1)
+        sum_begin(1, 1)
+        sum_second(1, 0)
+        out_product(0, 1)
+        sum_middle(1, 1)
+        output_low(0, 1)
+        output_delta(0, 0)
 
     sum_end(1, 0)
     sum_second(1, 1)
@@ -764,21 +789,24 @@
 
     @pl.when(s == 1)
     def _():
-        output_delta(0)
+        output_delta(0, 1)
 
     gather_end(1, 0)
     gather_middle(1, 1)
     drain(ring_copies(gathers[0]))
     down_product(1, 0)
     out_product(1, 0)
-    drain([other_down] + lows[0] + tops[0][0] + tops[0][1] + panels[0] + panels[1])
+    output_low(1, 0)
+    drain([other_down] + lows[0][0] + lows[0][1] + panels[0] + panels[1])
+    drain(tops[0][0] + tops[0][1])
     gather_end(1, 1)
     down_product(1, 1)
     out_product(1, 1)
-    output_low(1)
+    output_delta(1, 0)
+    output_low(1, 1)
     drain(ring_copies(rings[1]))
     drain(ring_copies(gathers[1]))
-    output_delta(1)
+    output_delta(1, 1)
     drain(list(started))
 
 
@@ -787,11 +815,12 @@
     second_out[...] = second_in[...]
 
 
-def on_device(*args):
+def on_device(hidden_input, fresh, *args):
+    rows = (RING, RING, 2, HALF_ROWS, FEAT)
     any_space = pl.BlockSpec(memory_space=pl.ANY)
     vmem = pl.BlockSpec(memory_space=pltpu.VMEM)
     smem = pl.BlockSpec(memory_space=pltpu.SMEM)
-    out = jax.ShapeDtypeStruct((1, 128, FEAT), BF16)
+    out = jax.ShapeDtypeStruct((1, RING, 2, HALF_ROWS, FEAT), BF16)
     v = pltpu.VMEM
     dma = pltpu.SemaphoreType.DMA
     first, second = pl.pallas_call(
@@ -830,22 +859,22 @@
             v((2, 2, RING, RING, HALF_ROWS, QCOLS), BF16),
             v((2, 2, RING, RING, HALF_ROWS, FEAT), BF16),
             v((2, 2, 3, RING, HALF_ROWS, FEAT), BF16),
-            v((2, ROWS, FEAT), BF16),
+            v((2, 2, RING, RING, HALF_ROWS, FEAT), BF16),
             v((ROWS // 2, FEAT), BF16),
             v((2, 2, 8, 256), jnp.int32),
-            v((2, RING, 8, 128), jnp.int32),
+            v((2, 2, RING, 8, 128), jnp.int32),
             v((OWN_ROWS * HEADS, HEAD), F32),
             v((OWN_ROWS * HEADS, HEAD), F32),
             v((OWN_ROWS * HEADS, HEAD), F32),
             v((OWN_ROWS * HEADS, HEAD), F32),
-            v((2, RING, RANK, 128), F32),
-            v((2, RING, RANK, 128), F32),
-            v((2, 16, RANK, 128), BF16),
+            v((2, 2, RING, RANK, 128), F32),
+            v((2, 2, RING, RANK, 128), F32),
+            v((2, 2, 16, RANK, 128), BF16),
             dma((N_SEM,)),
             dma((N_SEM,)),
-            dma((9,)),
-            dma((2, 16)),
-            dma((2, 16)),
+            dma((11,)),
+            dma((2, 2, 16)),
+            dma((2, 2, 16)),
             pltpu.SemaphoreType.REGULAR,
         ],
         compiler_params=pltpu.CompilerParams(
@@ -854,13 +883,14 @@
         cost_estimate=pl.CostEstimate(
             flops=8_000_000_000, bytes_accessed=16_000_000, transcendentals=500_000
         ),
-    )(*args)
-    return pl.pallas_call(
+    )(hidden_input.reshape(rows), fresh.reshape(rows), *args)
+    first, second = pl.pallas_call(
         hand_over,
         out_shape=(out, out),
         in_specs=[vmem, vmem],
         out_specs=(vmem, vmem),
     )(first, second)
+    return first.reshape(1, 128, FEAT), second.reshape(1, 128, FEAT)
 
 
 def solution(mesh):

time: 110 us -> 110 us (level)
  no operation moved by 1% of the time
where the time goes in v4:
time: 110 us; the launch traced here: 109 us
  Pallas kernels  109 us (99%)
    pallas_call x1, Pallas kernels, on_device(): pl.pallas_call(kernel, out_shape=(out, out), in_specs=[any_space, any_spa...  107 us

profile of v4, /device:TPU:1, one launch (start us, length us, event | category | flops | bytes accessed | tf_op | source)
XLA Modules:
  0.0 109.4 jit_solution(5745129344132961731)
XLA Ops:
  0.6 107.0 %shard_map.140 = (bf16[1,4,2,16,512]{4,3,2,1,0:T(8,128)(2,1)}, bf16[1,4,2,16,512]{4,3,2,1,0:T(8,128)(2,1)}) custom-call(bf16[4,4,2,16,512]{4,3,2,1,0:T(8,128)(2,1)} %bitcast.4, bf16[4,4,2,16,512]{4,3,2,1,0:T(8,128)(2,1)} %bitcast.5, f32[1,512]{1,0:T(1,128)} %gain_ref.1, bf16[1,512,2048]{2,1,0:T(8,128)(2,1)} %wq_hbm.1, bf16[1,512,2,256]{3,2,1,0:T(2,128)(2,1)} %wkv_hbm.1, ...), custom_call_target="tpu_custom_call" | custom-call | flops 8000000000 | bytes 16000000 | tf_op jit(solution)/shard_map/pallas_call | solution.py:826
  107.7 1.7 %shard_map.141 = (bf16[1,4,2,16,512]{4,3,2,1,0:T(8,128)(2,1)}, bf16[1,4,2,16,512]{4,3,2,1,0:T(8,128)(2,1)}) custom-call(bf16[1,4,2,16,512]{4,3,2,1,0:T(8,128)(2,1)} %get-tuple-element.6.first_in, bf16[1,4,2,16,512]{4,3,2,1,0:T(8,128)(2,1)} %get-tuple-element.7.second_in), custom_call_target="tpu_custom_call" | custom-call | tf_op jit(solution)/shard_map/pallas_call | solution.py:887

commit v5 on v4

--- a/solution.py
+++ b/solution.py
@@ -659,6 +659,7 @@
         project(0, 1)
         sum_middle(0, 0)
         sum_begin(0, 1)
+        pl.semaphore_signal(turn, inc=1, device_id={"section": o}, device_id_type=MESH)
         offs = slots_and_offsets()
         sum_middle(0, 1)
         sum_second(0, 0)
@@ -683,10 +684,6 @@
 
     sum_end(0, 0)
     sum_second(0, 1)
-
-    @pl.when(s == 0)
-    def _():
-        pl.semaphore_signal(turn, inc=1, device_id={"section": o}, device_id_type=MESH)
 
     load_c[0].wait()
     attention(0, 0)

time: 110 us -> 112 us (1.018)
  Pallas kernels: 109 us -> 111 us
    pallas_call x1, Pallas kernels: 107 us -> 109 us  [on_device(): pl.pallas_call(kernel, out_shape=(out, out), in_specs=[any_space, any_spa...]
where the time goes in v5:
time: 112 us
  Pallas kernels  111 us (99%)
    pallas_call x1, Pallas kernels, on_device(): pl.pallas_call(kernel, out_shape=(out, out), in_specs=[any_space, any_spa...  109 us

profile of v5, /device:TPU:1, one launch (start us, length us, event | category | flops | bytes accessed | tf_op | source)
XLA Modules:
  0.0 111.7 jit_solution(13980113019046766199)
XLA Ops:
  0.6 109.3 %shard_map.140 = (bf16[1,4,2,16,512]{4,3,2,1,0:T(8,128)(2,1)}, bf16[1,4,2,16,512]{4,3,2,1,0:T(8,128)(2,1)}) custom-call(bf16[4,4,2,16,512]{4,3,2,1,0:T(8,128)(2,1)} %bitcast.4, bf16[4,4,2,16,512]{4,3,2,1,0:T(8,128)(2,1)} %bitcast.5, f32[1,512]{1,0:T(1,128)} %gain_ref.1, bf16[1,512,2048]{2,1,0:T(8,128)(2,1)} %wq_hbm.1, bf16[1,512,2,256]{3,2,1,0:T(2,128)(2,1)} %wkv_hbm.1, ...), custom_call_target="tpu_custom_call" | custom-call | flops 8000000000 | bytes 16000000 | tf_op jit(solution)/shard_map/pallas_call | solution.py:823
  110.0 1.7 %shard_map.141 = (bf16[1,4,2,16,512]{4,3,2,1,0:T(8,128)(2,1)}, bf16[1,4,2,16,512]{4,3,2,1,0:T(8,128)(2,1)}) custom-call(bf16[1,4,2,16,512]{4,3,2,1,0:T(8,128)(2,1)} %get-tuple-element.6.first_in, bf16[1,4,2,16,512]{4,3,2,1,0:T(8,128)(2,1)} %get-tuple-element.7.second_in), custom_call_target="tpu_custom_call" | custom-call | tf_op jit(solution)/shard_map/pallas_call | solution.py:884
